TPU v7x, 256 devices: a whole 4x4x8 slice. The times are simulated.
256 devices in a mesh: ctx: 64 (over z, x, core), head: 4 (over y).
Axes of the slice: x: 4, y: 4, z: 8, core: 2. Of those that a mesh axis runs over, the one named last changes fastest.
Arguments:
- queries: bfloat16 [65536, 4096], P('ctx', 'head'), may hold values from -6 to 6
- keys: bfloat16 [65536, 4096], P('ctx', 'head'), may hold values from -0.059814453 to 0.059814453
- values: bfloat16 [65536, 4096], P('ctx', 'head'), may hold values from -40 to 40
- log_decay: float32 [32, 65536], P('head', 'ctx'), may hold values from -1 to 0
- out_gain: float32 [4096], P('head'), may hold values from 0.1 to 1.9
- decode_map: int32 [256], P(('ctx', 'head')), may hold values from 0 to 255, each once
Outputs:
- out: bfloat16 [65536, 4096], P('ctx', 'head')
- decode_state: float32 [4096, 128], P(('ctx', 'head'))
Inputs may be any that keep to these rules, and one draw needn't show every extreme that they name: `decode_map`: each slot names a different block.
All inputs are finite; a program needn't handle non-finite values.
Results may differ from a plain program's by a relative error of at most 0.0036.
Values sent between devices are 32-bit elements; how exact they have to be, the bound alone decides.
No kernel may reach another device: no remote copies, remote signals or barrier semaphores. Data moves between devices by JAX's collectives and lax.ppermute only.
A program may use at most 128 MiB of HBM per device.

v0:
```python
import jax
import jax.numpy as jnp
from jax import lax
from jax.sharding import PartitionSpec as P

BLK = 256


exact_mode = lax.Precision.HIGHEST


def compose_rows(parts):
    decays, states = parts

    def joined(early, late):
        return (early[0] + late[0], jnp.exp(late[0])[..., None] * early[1] + late[1])

    running = lax.associative_scan(joined, (decays, states), axis=1)
    before = jnp.concatenate([jnp.zeros_like(states[:, :1]), running[1][:, :-1]], axis=1)
    return (before, running[1][:, -1:])


def block_local(parts, heads, size):
    q_block, k_block, v_block, cum_block = parts
    length = q_block.shape[0]
    positions = jnp.arange(length)
    causal = positions[:, None] >= positions[None, :]
    pieces = []
    for head_index in range(heads):
        first_col = head_index * size
        last_col = first_col + size
        scores = jnp.einsum(
            "td,sd->ts",
            q_block[:, first_col:last_col],
            k_block[:, first_col:last_col],
            preferred_element_type=jnp.float32,
        )
        gap = cum_block[head_index][:, None] - cum_block[head_index][None, :]
        weights = jnp.where(causal, jnp.exp(jnp.where(causal, gap, 0.0)), 0.0)
        probs = (scores * weights).astype(jnp.bfloat16)
        pieces.append(
            jnp.dot(probs, v_block[:, first_col:last_col], preferred_element_type=jnp.float32)
        )
    return jnp.concatenate(pieces, axis=1)


def per_device(queries, keys, values, log_decay, out_gain, decode_map):
    tok_count, width = queries.shape
    heads = log_decay.shape[0]
    size = width // heads
    blocks = tok_count // BLK
    decay_blocks = log_decay.reshape(heads, blocks, BLK)
    cum = jnp.cumsum(decay_blocks, axis=2)
    totals = cum[:, :, -1]
    k_float = keys.reshape(blocks, BLK, heads, size).astype(jnp.float32)
    v_float = values.reshape(blocks, BLK, heads, size).astype(jnp.float32)
    weighted = k_float * jnp.exp(totals[:, :, None] - cum).transpose(1, 2, 0)[..., None]
    gsum = jnp.einsum("nshd,nshe->nhde", weighted, v_float, precision=exact_mode)
    starts = []
    running = jnp.zeros((heads, size, size), jnp.float32)
    for block_index in range(blocks):
        starts.append(running)
        running = jnp.exp(totals[:, block_index])[:, None, None] * running + gsum[block_index]
    shard_quantity = jnp.sum(totals, axis=1)
    ctx_count = lax.axis_size("ctx")
    head_count = lax.axis_size("head")
    owner_rows = heads * size // ctx_count
    rows_state = running.reshape(ctx_count, 1, owner_rows, size)
    rows_decay = jnp.broadcast_to(shard_quantity[:, None], (heads, size)).reshape(
        ctx_count, 1, owner_rows
    )
    before, last_rows = compose_rows(
        (
            lax.all_to_all(rows_decay, "ctx", split_axis=0, concat_axis=1, tiled=True),
            lax.all_to_all(rows_state, "ctx", split_axis=0, concat_axis=1, tiled=True),
        )
    )
    returned = lax.all_to_all(before, "ctx", split_axis=1, concat_axis=0, tiled=True)
    received_state = returned.reshape(heads, size, size)
    gathered = lax.all_gather(last_rows[0, 0], ("ctx", "head"), axis=0, tiled=True)
    wanted = decode_map[0]
    position = wanted % ctx_count * head_count + wanted // ctx_count
    decode_state = lax.dynamic_slice_in_dim(gathered, position * owner_rows, owner_rows, 0)
    q_blocks = queries.reshape(blocks, BLK, width)
    k_blocks = keys.reshape(blocks, BLK, width)
    v_blocks = values.reshape(blocks, BLK, width)
    cum_by_block = cum.transpose(1, 0, 2)
    local = lax.map(
        lambda parts: block_local(parts, heads, size), (q_blocks, k_blocks, v_blocks, cum_by_block)
    )
    q_float = queries.reshape(blocks, BLK, heads, size).astype(jnp.float32)
    cum_tokens = cum.transpose(1, 2, 0)
    offsets = (jnp.cumsum(totals, axis=1) - totals).T
    initial_state_stack = jnp.stack(starts)
    effective = initial_state_stack + jnp.exp(offsets)[:, :, None, None] * received_state[None]
    carried = (
        jnp.einsum("nthd,nhde->nthe", q_float, effective, precision=exact_mode)
        * jnp.exp(cum_tokens)[..., None]
    )
    attn = local.reshape(blocks, BLK, heads, size) + carried
    mean_sq = jnp.mean(attn * attn, axis=-1, keepdims=True)
    normed = attn * lax.rsqrt(mean_sq + 1e-05) * out_gain.reshape(heads, size)
    return (normed.reshape(tok_count, width).astype(jnp.bfloat16), decode_state)


def solution(mesh):
    return jax.shard_map(
        per_device,
        mesh=mesh,
        in_specs=(
            P("ctx", "head"),
            P("ctx", "head"),
            P("ctx", "head"),
            P("head", "ctx"),
            P("head"),
            P(("ctx", "head")),
        ),
        out_specs=(P("ctx", "head"), P(("ctx", "head"), None)),
        check_vma=False,
    )
```

profile of v0, /device:TPU:32, one launch (start us, length us, event | category | flops | bytes accessed | tf_op | source)
XLA Modules:
  0.0 209.5 jit_solution(14256230446302092052)
XLA Ops:
  7.9 2.3 %reduce-window.6 = f32[8,4,2,128]{3,0,1,2:T(8,128)S(1)} reduce-window(f32[8,4,2,128]{3,0,1,2:T(8,128)S(1)} %copy.20, f32[]{:T(128)} %constant.54.clone.1), window={size=1x1x1x128 pad=0_0x0_0x0_0x127_0}, to_apply=%region_0.0 | reduce-window | flops 1040384 | bytes 65540 | tf_op jit(solution)/shard_map/reduce-window
  11.6 11.6 %all-to-all-start.1 = ((f32[64,1,16]{2,1,0:T(1,128)}), f32[64,1,16]{2,1,0:T(1,128)S(1)}, u32[]{:S(2)}, u32[]{:S(2)}) async-start(f32[64,1,16]{2,1,0:T(1,128)} %broadcast_in_dim.65), calls=%async_computation.1 | async-start | bytes 65536 | tf_op jit(solution)/shard_map/all_to_all | solution.py:74
  23.3 2.0 convert_bitcast_fusion
  25.3 3.0 %copy.34 = f32[128,8,8,128]{3,2,1,0:T(8,128)} copy(f32[128,8,8,128]{3,1,2,0:T(8,128)S(1)} %convert_bitcast_fusion) | data formatting | bytes 8388608
  28.3 5.3 %copy.22 = f32[4,256,8,128]{1,3,2,0:T(8,128)} copy(f32[4,256,8,128]{3,2,1,0:T(8,128)} %bitcast.139) | data formatting | bytes 8388608 | tf_op jit(solution)/shard_map/convert_element_type | solution.py:55
  33.6 2.2 %copy.35 = bf16[128,8,8,128]{3,2,1,0:T(8,128)(2,1)S(1)} copy(bf16[128,8,8,128]{3,1,2,0:T(8,128)(2,1)} %bitcast.62) | data formatting | bytes 4194304
  36.1 4.8 %fusion.113 = f32[4,8,128,128]{3,2,1,0:T(8,128)S(1)} fusion(f32[4,256,8,128]{1,3,2,0:T(8,128)} %copy.22, bf16[4,256,8,128]{3,2,1,0:T(8,128)(2,1)S(1)} %bitcast.144, f32[4,256,8]{1,2,0:T(8,128)S(1)} %get-tuple-element.69), kind=kOutput, calls=%fused_computation.130 | convolution fusion | flops 1611661312 | bytes 8421376 | tf_op jit(solution)/shard_map/nshd,nshe->nhde/dot_general | solution.py:58
  40.9 1.3 multiply_add_fusion.1
  42.5 1.1 multiply_add_fusion
  43.6 10.3 %all-to-all-start = ((f32[64,1,16,128]{3,2,1,0:T(8,128)}), f32[64,1,16,128]{3,2,1,0:T(8,128)S(1)}, u32[]{:S(2)}, u32[]{:S(2)}) async-start(f32[64,1,16,128]{3,2,1,0:T(8,128)} %multiply_add_fusion), calls=%async_computation | async-start | bytes 1048576 | tf_op jit(solution)/shard_map/all_to_all | solution.py:75
  54.3 16.4 %all-to-all-done = f32[64,1,16,128]{3,2,1,0:T(8,128)S(1)} async-done(((f32[64,1,16,128]{3,2,1,0:T(8,128)}), f32[64,1,16,128]{3,2,1,0:T(8,128)S(1)}, u32[]{:S(2)}, u32[]{:S(2)}) %all-to-all-start) | async-done | bytes 524320 | tf_op jit(solution)/shard_map/all_to_all | solution.py:75
  72.6 10.3 %pad.102 = f32[1,63,16,128]{3,2,1,0:T(8,128)} pad(f32[1,32,16,128]{3,2,1,0:T(8,128)S(1)} %add.201, f32[]{:T(128)} %constant.54.clone.1), padding=0_0_0x0_0_1x0_0_0x0_0_0 | pad | bytes 778244
  84.2 6.9 %all-to-all-start.2 = ((f32[1,64,16,128]{3,2,0,1:T(8,128)}), f32[1,64,16,128]{3,2,0,1:T(8,128)}, u32[]{:S(2)}, u32[]{:S(2)}) async-start(f32[1,64,16,128]{3,2,0,1:T(8,128)} %pad_bitcast_fusion), calls=%async_computation.2 | async-start | bytes 1048576 | tf_op jit(solution)/shard_map/all_to_all | solution.py:78
  91.3 1.3 slice.507
  92.6 25.8 %while.10 = (s32[]{:T(128)}, f32[4,256,1024]{1,2,0:T(8,128)}, bf16[4,256,1024]{2,1,0:T(8,128)(2,1)}, bf16[4,256,1024]{2,1,0:T(8,128)(2,1)}, f32[4,8,256]{2,1,0:T...) while((s32[]{:T(128)}, f32[4,256,1024]{1,2,0:T(8,128)}, ...), condition=%wide.region_3.4_spmd, body=%wide.region_2.3_spmd.sunk | while | flops 271581184 | bytes 7897865 | solution.py:88
  92.7 1.3 dynamic-slice_bitcast_fusion.6
  93.9 1.1 dynamic-slice_bitcast_fusion.7
  99.1 1.3 dynamic-slice_bitcast_fusion.6
  100.3 1.1 dynamic-slice_bitcast_fusion.7
  104.4 1.1 bitcast_dynamic-update-slice_fusion.2
  105.5 1.3 dynamic-slice_bitcast_fusion.6
  106.8 1.1 dynamic-slice_bitcast_fusion.7
  110.9 1.1 bitcast_dynamic-update-slice_fusion.2
  112.0 1.3 dynamic-slice_bitcast_fusion.6
  113.3 1.1 dynamic-slice_bitcast_fusion.7
  119.1 2.3 %copy.36 = bf16[128,8,8,128]{3,2,1,0:T(8,128)(2,1)S(1)} copy(bf16[128,8,8,128]{3,1,2,0:T(8,128)(2,1)} %bitcast.141) | data formatting | bytes 4194304
  121.5 5.4 %multiply_reduce_fusion = (f32[4,256,8]{1,2,0:T(8,128)S(1)}, f32[4,256,8,128]{1,3,2,0:T(8,128)S(1)}) fusion(f32[4,256,8,128]{1,3,2,0:T(8,128)} %bitcast.145, f32[4,256,8]{1,2,0:T(8,128)S(1)} %get-tuple-element.68, bf16[4,256,8,128]{3,2,1,0:T(8,128)(2,1)S(1)} %bitcast.143, f32[1,8,128,128]{3,2,1,0:T(8,128)S(1)} %get-tuple-element.49, ...), kind=kOutput, calls=%fused_computation.129 | convolution fusion | flops 1617420288 | bytes 12648592 | tf_op jit(solution)/shard_map/nthd,nhde->nthe/dot_general | solution.py:97
  126.9 1.9 multiply_convert_fusion
  128.8 3.1 %copy.31 = bf16[4,256,8,128]{3,2,1,0:T(8,128)(2,1)S(1)} copy(bf16[4,256,8,128]{1,3,2,0:T(8,128)(2,1)} %multiply_convert_fusion) | data formatting | bytes 4194304 | tf_op jit(solution)/shard_map/convert_element_type | solution.py:103
  132.0 1.9 copy.52
  133.9 67.5 %all-gather.3.cloned.1.call-done = f32[1,1,4096,128]{3,2,1,0:T(8,128)} async-done(((f32[1,1,16,128]{3,2,1,0:T(8,128)}), f32[1,1,4096,128]{3,2,1,0:T(8,128)}) %all-gather.3.cloned.1.call-update) | async-done | bytes 2097168 | tf_op jit(solution)/shard_map/all_gather | solution.py:80
  201.4 1.3 dynamic-slice_bitcast_fusion.3
  (132 shorter events, 20.4 us)
Async XLA Ops:
  11.6 32.0 %all-to-all-start.1 = ((f32[64,1,16]{2,1,0:T(1,128)}), f32[64,1,16]{2,1,0:T(1,128)S(1)}, u32[]{:S(2)}, u32[]{:S(2)}) async-start(f32[64,1,16]{2,1,0:T(1,128)} %broadcast_in_dim.65), calls=%async_computation.1 | async-start | bytes 65536 | tf_op jit(solution)/shard_map/all_to_all | solution.py:74
  43.6 27.1 %all-to-all-start = ((f32[64,1,16,128]{3,2,1,0:T(8,128)}), f32[64,1,16,128]{3,2,1,0:T(8,128)S(1)}, u32[]{:S(2)}, u32[]{:S(2)}) async-start(f32[64,1,16,128]{3,2,1,0:T(8,128)} %multiply_add_fusion), calls=%async_computation | async-start | bytes 1048576 | tf_op jit(solution)/shard_map/all_to_all | solution.py:75
  84.2 37.3 %all-to-all-start.2 = ((f32[1,64,16,128]{3,2,0,1:T(8,128)}), f32[1,64,16,128]{3,2,0,1:T(8,128)}, u32[]{:S(2)}, u32[]{:S(2)}) async-start(f32[1,64,16,128]{3,2,0,1:T(8,128)} %pad_bitcast_fusion), calls=%async_computation.2 | async-start | bytes 1048576 | tf_op jit(solution)/shard_map/all_to_all | solution.py:78
  91.1 110.3 %all-gather.3.cloned.1.call-start = ((), (), s32[]{:S(2)}) async-start(), calls=%async_computation.3 | async-start | bytes 2105344 | tf_op jit(solution)/shard_map/all_gather | solution.py:80
  119.1 2.4 %copy-start = (f32[1,8,128,128]{3,2,1,0:T(8,128)S(1)}, f32[1,8,128,128]{3,2,1,0:T(8,128)}, u32[]{:S(2)}) copy-start(f32[1,8,128,128]{3,2,1,0:T(8,128)} %get-tuple-element.50) | copy-start | bytes 1572868
  121.5 5.4 %copy-start.1 = (f32[1024]{0:T(1024)S(1)}, f32[1024]{0:T(1024)}, u32[]{:S(2)}) copy-start(f32[1024]{0:T(1024)} %param.12) | copy-start | bytes 12292
Sparse Core Ops, SparseCore 0:
  96.2 105.1 all-gather.2
where the time goes:
time: 212 us; the launch traced here: 210 us
  waiting for transfers between devices  83.9 us (40%)
  local copies, waits for them, and re-layouts  49 us (23%)
  starting transfers between devices  29 us (14%)
  matrix products  21.9 us (10%)
  between operations  15.2 us (7%)
  other arithmetic  10.3 us (5%)
    all_gather x1, waiting for transfers between devices, per_device(): lax.all_gather(last_rows[0, 0], ('ctx', 'head'), axis=0, tiled=True)  67.5 us
    unnamed x9, local copies, waits for them, and re-layouts  19.7 us
    all_to_all x1, waiting for transfers between devices, per_device(): lax.all_to_all(rows_state, 'ctx', split_axis=0, concat_axis=1, tiled=True)  16.4 us
    dot_general x32, matrix products, block_local(): jnp.dot(probs, v_block[:, first_col:last_col], preferred_element_type=jnp...  11.7 us
    all_to_all x1, starting transfers between devices, per_device(): lax.all_to_all(rows_decay, 'ctx', split_axis=0, concat_axis=1, tiled=True)  11.6 us
    all_to_all x1, starting transfers between devices, per_device(): lax.all_to_all(rows_state, 'ctx', split_axis=0, concat_axis=1, tiled=True)  10.3 us
    squeeze x8, local copies, waits for them, and re-layouts, per_device(): lax.map(lambda parts: block_local(parts, heads, size), (q_blocks, k_block...  9.41 us
    all_to_all x1, starting transfers between devices, per_device(): lax.all_to_all(before, 'ctx', split_axis=1, concat_axis=0, tiled=True)  6.87 us
  transfers between devices with their start and end apart: 4, of which 2 were waited for; matrix products, arithmetic and copies ran while one was open for 30% of the time, Pallas kernels for 0%

commit v1 on v0

v1 whole, which is shorter than its diff:
```python
import functools

import jax
import jax.numpy as jnp
from jax import lax
from jax.experimental import pallas as pl
from jax.experimental.pallas import tpu as pltpu
from jax.sharding import PartitionSpec as P

BLK = 256
EXT = 8
f32 = jnp.float32
bf16 = jnp.bfloat16
SMEM = pl.BlockSpec(memory_space=pltpu.SMEM)
VMEM = pl.BlockSpec(memory_space=pltpu.VMEM)
PARAMS = pltpu.CompilerParams(vmem_limit_bytes=40 * 1024 * 1024)


def dot(a, b):
    return lax.dot_general(a, b, (((1,), (0,)), ((), ())), preferred_element_type=f32)


def split2(x):
    hi = x.astype(bf16)
    return hi, (x - hi.astype(f32)).astype(bf16)


def split3(x):
    hi = x.astype(bf16)
    rest = x - hi.astype(f32)
    mid = rest.astype(bf16)
    return hi, mid, (rest - mid.astype(f32)).astype(bf16)


def block_cums(ld):
    heads, tokens = ld.shape
    n = tokens // BLK
    row = lax.broadcasted_iota(jnp.int32, (BLK, BLK), 0)
    col = lax.broadcasted_iota(jnp.int32, (BLK, BLK), 1)
    tri = jnp.where(row <= col, 1.0, 0.0).astype(bf16)
    parts = []
    for j in range(n):
        parts += list(split3(ld[:, j * BLK : (j + 1) * BLK].astype(f32)))
    stacked = jnp.concatenate([p.astype(f32) for p in parts], axis=0).astype(bf16)
    sums = dot(stacked, tri)
    out = []
    for j in range(n):
        a = sums[(3 * j) * heads : (3 * j + 1) * heads]
        b = sums[(3 * j + 1) * heads : (3 * j + 2) * heads]
        c = sums[(3 * j + 2) * heads : (3 * j + 3) * heads]
        out.append(a + (b + c))
    return out


def summary_kernel(first, idx_ref, k_ref, v_ref, ld_ref, s_ref, w_ref, tot_ref):
    step = pl.program_id(0)
    heads, tokens = ld_ref.shape
    n = tokens // BLK
    half = heads // 2

    @pl.when(step == 0)
    def _():
        cums = block_cums(ld_ref[...])
        after = jnp.zeros((heads, 1), f32)
        for j in reversed(range(n)):
            total = cums[j][:, BLK - 1 : BLK]
            w_ref[:, j * BLK : (j + 1) * BLK] = jnp.exp(total - cums[j] + after)
            after = after + total
        tot_ref[...] = jnp.broadcast_to(after, tot_ref.shape)

    core = idx_ref[0]
    head = step + half * ((1 - core) if first else core)
    w = w_ref[pl.ds(head, 1), :]
    kt = k_ref[...].T.astype(f32) * w
    hi, lo = split2(kt)
    v = v_ref[...]
    s_ref[0, 0:128, :] = dot(hi, v) + dot(lo, v)
    s_ref[0, 128:136, :] = jnp.broadcast_to(tot_ref[pl.ds(head, 1), :], (EXT, 128))


def summary(first, idx, keys, values, ld):
    tokens, width = keys.shape
    heads = ld.shape[0]
    half = heads // 2

    def col(i, idx):
        return (0, i + half * ((1 - idx[0]) if first else idx[0]))

    return pl.pallas_call(
        functools.partial(summary_kernel, first),
        out_shape=jax.ShapeDtypeStruct((half, 128 + EXT, 128), f32),
        grid_spec=pltpu.PrefetchScalarGridSpec(
            num_scalar_prefetch=1,
            grid=(half,),
            in_specs=[
                pl.BlockSpec((tokens, 128), col),
                pl.BlockSpec((tokens, 128), col),
                pl.BlockSpec((heads, tokens), lambda i, idx: (0, 0)),
            ],
            out_specs=pl.BlockSpec((1, 128 + EXT, 128), lambda i, idx: (i, 0, 0)),
            scratch_shapes=[pltpu.VMEM((heads, tokens), f32), pltpu.VMEM((heads, 128), f32)],
        ),
        compiler_params=PARAMS,
        cost_estimate=pl.CostEstimate(flops=2 * 2 * half * tokens * 128 * 128, bytes_accessed=2 * tokens * width, transcendentals=0),
        name="summary_a" if first else "summary_b",
    )(idx, keys, values, ld)


def compose(early, late):
    scale = jnp.exp(late[1])
    return (scale[0:1] * early[0] + late[0], early[1] + late[1])


def parts(ref):
    return (ref[0:128, :], ref[128:136, :])


def pair_kernel(idx_ref, keep_ref, recv_ref, *outs):
    core, x = idx_ref[0], idx_ref[1]
    for d in range(4):
        j = x ^ d
        own = (keep_ref[j, 0:128, :], keep_ref[j, 128:136, :])
        got = (recv_ref[j, 0:128, :], recv_ref[j, 128:136, :])
        zero = core == 0
        early = tuple(jnp.where(zero, a, b) for a, b in zip(own, got))
        late = tuple(jnp.where(zero, b, a) for a, b in zip(own, got))
        state, decay = compose(early, late)
        outs[d][0:128, :] = state
        outs[d][128:136, :] = decay


def pick(x, j, refs):
    state, decay = parts(refs[0])
    for d in range(1, 4):
        here = (x ^ d) == j
        s, e = parts(refs[d])
        state, decay = jnp.where(here, s, state), jnp.where(here, e, decay)
    return state, decay


def slab_kernel(idx_ref, t0, t1, t2, t3, u_ref):
    x = idx_ref[1]
    refs = (t0, t1, t2, t3)
    total = pick(x, 0, refs)
    for j in range(1, 4):
        total = compose(total, pick(x, j, refs))
    u_ref[0:128, :] = total[0]
    u_ref[128:136, :] = total[1]


def round_kernel(bit, idx_ref, g_ref, r_ref, a_ref, g_out, a_out):
    late = idx_ref[bit] == 1
    g, r, a = parts(g_ref), parts(r_ref), parts(a_ref)
    early_part = tuple(jnp.where(late, p, q) for p, q in zip(r, g))
    late_part = tuple(jnp.where(late, p, q) for p, q in zip(g, r))
    state, decay = compose(early_part, late_part)
    g_out[0:128, :] = state
    g_out[128:136, :] = decay
    state, decay = compose(r, a)
    a_out[0:128, :] = jnp.where(late, state, a[0])
    a_out[128:136, :] = jnp.where(late, decay, a[1])


def back_kernel(idx_ref, g_ref, a_ref, t0, t1, t2, t3, *outs):
    x = idx_ref[1]
    refs = (t0, t1, t2, t3)
    before = [parts(a_ref)]
    for j in range(3):
        before.append(compose(before[-1], pick(x, j, refs)))
    for d in range(4):
        j = x ^ d
        state = before[0][0]
        for i in range(1, 4):
            state = jnp.where(j == i, before[i][0], state)
        outs[d][0:128, :] = state
        outs[d][128:256, :] = g_ref[0:128, :]


def spread_kernel(idx_ref, want_ref, m0, m1, m2, m3, keep_ref, recv_ref, own_ref, send_ref, slot_send, slot_keep):
    core, x, y = idx_ref[0], idx_ref[1], idx_ref[5]
    zero = core == 0
    refs = (m0, m1, m2, m3)
    for d in range(4):
        j = x ^ d
        chip = refs[d][0:128, :]
        s0 = jnp.where(zero, keep_ref[j, 0:128, :], recv_ref[j, 0:128, :])
        l0 = jnp.where(zero, keep_ref[j, 128:129, :], recv_ref[j, 128:129, :])
        second = jnp.exp(l0) * chip + s0
        own_ref[j] = jnp.where(zero, chip, second)
        send_ref[j] = jnp.where(zero, second, chip)
    for slot in range(8):
        want = want_ref[slot]
        mine = (want // 32) == (y * 2 + core)
        chip = ((want // 8) % 4) ^ x
        row = pl.multiple_of(128 + (want % 8) * 16, 16)
        rows = m0[pl.ds(row, 16), :]
        for d in range(1, 4):
            rows = jnp.where(chip == d, refs[d][pl.ds(row, 16), :], rows)
        rows = jnp.where(mine, rows, 0.0)
        if slot in (2, 3):
            slot_send[slot - 2] = rows
        elif slot in (6, 7):
            slot_send[slot - 4] = rows
        elif slot in (0, 1):
            slot_keep[slot] = rows
        else:
            slot_keep[slot - 2] = rows


def small(kernel, outs, name):
    def call(*args):
        n = args[0].size
        specs = [SMEM if a.dtype == jnp.int32 else VMEM for a in args]
        return pl.pallas_call(
            kernel,
            out_shape=[jax.ShapeDtypeStruct(s, f32) for s in outs],
            in_specs=specs,
            out_specs=[VMEM] * len(outs),
            compiler_params=PARAMS,
            name=name,
        )(*args)

    return call


def local_kernel(base, q_ref, k_ref, v_ref, ld_ref, attn_ref, e_ref, run_ref, off_ref):
    step = pl.program_id(0)
    count = q_ref.shape[1] // 128

    @pl.when(step == 0)
    def _():
        run_ref[...] = jnp.zeros_like(run_ref)
        off_ref[...] = jnp.zeros_like(off_ref)

    cum = block_cums(ld_ref[...])[0]
    total = cum[:, BLK - 1 : BLK]
    cum_t = cum.T
    e_in = jnp.exp(cum_t)
    off = off_ref[...]
    e_ref[...] = jnp.exp((cum + off[:, 0:1]).T)
    off_ref[...] = off + total
    tail = jnp.exp(total - cum)
    h2 = BLK // 2
    row = lax.broadcasted_iota(jnp.int32, (h2, h2), 0)
    col = lax.broadcasted_iota(jnp.int32, (h2, h2), 1)
    causal = row >= col
    for i in range(count):
        h = base + i
        cols = slice(i * 128, (i + 1) * 128)
        q, k, v = q_ref[:, cols], k_ref[:, cols], v_ref[:, cols]
        kt = k.T
        c_row = cum[h : h + 1, :]
        c_col = cum_t[:, h : h + 1]
        run = run_ref[i]
        hi, lo = split2(run)
        carried = dot(jnp.concatenate([q, q], axis=1), jnp.concatenate([hi, lo], axis=0))
        carried = carried * e_in[:, h : h + 1]
        for t in range(2):
            rows = slice(t * h2, (t + 1) * h2)
            scores = dot(q[rows], kt[:, : (t + 1) * h2])
            gap = c_col[rows] - c_row[:, rows]
            diag = jnp.where(causal, jnp.exp(jnp.where(causal, gap, 0.0)), 0.0) * scores[:, rows]
            if t == 0:
                probs = diag
            else:
                gap = c_col[rows] - c_row[:, :h2]
                probs = jnp.concatenate([jnp.exp(gap) * scores[:, :h2], diag], axis=1)
            attn_ref[rows, cols] = dot(probs.astype(bf16), v[: (t + 1) * h2]) + carried[rows]
        khi, klo = split2(kt.astype(f32) * tail[h : h + 1, :])
        run_ref[i] = run * jnp.exp(total[h : h + 1, :]) + (dot(khi, v) + dot(klo, v))


def local_part(part, count, queries, keys, values, ld):
    tokens, _ = keys.shape
    heads = ld.shape[0]
    tile = pl.BlockSpec((BLK, 128 * count), lambda j: (j, part))
    return pl.pallas_call(
        functools.partial(local_kernel, part * count),
        out_shape=[jax.ShapeDtypeStruct((tokens, 128 * count), f32), jax.ShapeDtypeStruct((tokens, heads), f32)],
        grid=(tokens // BLK,),
        in_specs=[tile, tile, tile, pl.BlockSpec((heads, BLK), lambda j: (0, j))],
        out_specs=[pl.BlockSpec((BLK, 128 * count), lambda j: (j, 0)), pl.BlockSpec((BLK, heads), lambda j: (j, 0))],
        scratch_shapes=[pltpu.VMEM((count, 128, 128), f32), pltpu.VMEM((heads, 128), f32)],
        compiler_params=PARAMS,
        cost_estimate=pl.CostEstimate(flops=count * tokens * 2 * 128 * (256 + 256 + 256), bytes_accessed=10 * tokens * 128 * count, transcendentals=count * tokens * 200),
        name="local_attn",
    )(queries, keys, values, ld)


def last_kernel(count, idx_ref, q_ref, e_ref, gain_ref, own_ref, recv_ref, *rest):
    attn_refs, out_ref, p_ref = rest[:-2], rest[-2], rest[-1]
    heads = p_ref.shape[0]
    half = heads // 2

    @pl.when(pl.program_id(0) == 0)
    def _():
        core = idx_ref[0]
        for h in range(heads):
            state = jnp.where(core == h // half, own_ref[h % half], recv_ref[h % half])
            hi, lo = split2(state)
            p_ref[h, 0:128, :] = hi
            p_ref[h, 128:256, :] = lo

    for h in range(heads):
        cols = slice(h * 128, (h + 1) * 128)
        q = q_ref[:, cols]
        sub = slice((h % count) * 128, (h % count + 1) * 128)
        carried = dot(jnp.concatenate([q, q], axis=1), p_ref[h])
        attn = attn_refs[h // count][:, sub] + carried * e_ref[:, h : h + 1]
        mean = jnp.mean(attn * attn, axis=1, keepdims=True)
        out_ref[:, cols] = (attn * lax.rsqrt(mean + 1e-5) * gain_ref[:, cols]).astype(bf16)


def last_part(count, idx, queries, e, gain, own, recv, attns):
    tokens, width = queries.shape
    heads = width // 128
    whole = pl.BlockSpec((heads // 2, 128, 128), lambda j: (0, 0, 0))
    return pl.pallas_call(
        functools.partial(last_kernel, count),
        out_shape=jax.ShapeDtypeStruct((tokens, width), bf16),
        grid=(tokens // BLK,),
        in_specs=[
            SMEM,
            pl.BlockSpec((BLK, width), lambda j: (j, 0)),
            pl.BlockSpec((BLK, heads), lambda j: (j, 0)),
            pl.BlockSpec((1, width), lambda j: (0, 0)),
            whole,
            whole,
        ]
        + [pl.BlockSpec((BLK, 128 * count), lambda j: (j, 0))] * len(attns),
        out_specs=pl.BlockSpec((BLK, width), lambda j: (j, 0)),
        scratch_shapes=[pltpu.VMEM((heads, 256, 128), bf16)],
        compiler_params=PARAMS,
        cost_estimate=pl.CostEstimate(flops=heads * tokens * 2 * 256 * 128, bytes_accessed=8 * tokens * width, transcendentals=tokens * heads),
        name="last",
    )(idx, queries, e, gain, own, recv, *attns)


def per_device(queries, keys, values, log_decay, out_gain, decode_map):
    ctx_size = lax.axis_size("ctx")
    head_size = lax.axis_size("head")

    def swap(a, mask):
        return lax.ppermute(a, "ctx", [(i, i ^ mask) for i in range(ctx_size)])

    def swap_y(a, mask):
        return lax.ppermute(a, "head", [(i, i ^ mask) for i in range(head_size)])

    at = lax.axis_index("ctx")
    y = lax.axis_index("head")
    core, x, z = at % 2, (at // 2) % 4, at // 8
    idx = jnp.stack([core, x, z & 1, (z >> 1) & 1, z >> 2, y]).astype(jnp.int32)

    ext = (128 + EXT, 128)
    send = summary(True, idx, keys, values, log_decay)
    recv = swap(send, 1)
    keep = summary(False, idx, keys, values, log_decay)

    w1 = jnp.concatenate([decode_map, swap(decode_map, 1)])
    w2 = jnp.concatenate([w1, swap_y(w1, 1)])
    want = jnp.concatenate([w2, swap_y(w2, 3)])

    t = small(pair_kernel, [ext] * 4, "pair")(idx, keep, recv)
    t = [t[0]] + [swap(t[d], 2 * d) for d in (1, 2, 3)]
    (g,) = small(slab_kernel, [ext], "slab")(idx, *t)
    a = jnp.zeros(ext, f32)
    for bit, mask in ((2, 8), (3, 16), (4, 48)):
        r = swap(g, mask)
        g, a = small(functools.partial(round_kernel, bit), [ext] * 2, "round")(idx, g, r, a)
    m = small(back_kernel, [(256, 128)] * 4, "back")(idx, g, a, *t)
    m = [m[0]] + [swap(m[d], 2 * d) for d in (1, 2, 3)]
    own, other, slot_send, slot_keep = small(
        spread_kernel, [(4, 128, 128)] * 2 + [(4, 16, 128)] * 2, "spread"
    )(idx, want, *m, keep, recv)
    other = swap(other, 1)

    slots = slot_keep + swap_y(slot_send, 1)
    slots = slots[0:2] + swap_y(slots[2:4], 3)
    decode_state = slots[0] + swap(slots[1], 1)

    count = 2
    locals_ = [local_part(i, count, queries, keys, values, log_decay) for i in range(8 // count)]
    out = last_part(
        count, idx, queries, locals_[0][1], out_gain.reshape(1, -1), own, other, [p[0] for p in locals_]
    )
    return (out, decode_state)


def solution(mesh):
    return jax.shard_map(
        per_device,
        mesh=mesh,
        in_specs=(
            P("ctx", "head"),
            P("ctx", "head"),
            P("ctx", "head"),
            P("head", "ctx"),
            P("head"),
            P(("ctx", "head")),
        ),
        out_specs=(P("ctx", "head"), P(("ctx", "head"), None)),
        check_vma=False,
    )
```

time: 212 us -> 83.1 us (0.39)
  waiting for transfers between devices: 83.9 us -> 13.4 us
  local copies, waits for them, and re-layouts: 49 us -> 4.06 us
  Pallas kernels: 0 us -> 34.6 us
  matrix products: 21.9 us -> 0 us
  between operations: 15.2 us -> 1.51 us
  other arithmetic: 10.3 us -> 2.54 us
  starting transfers between devices: 29 us -> 26.2 us
    all_gather x1 -> x0, waiting for transfers between devices: 67.5 us -> none  [per_device(): lax.all_gather(last_rows[0, 0], ('ctx', 'head'), axis=0, tiled=True)]
    pallas_call x0 -> x14, Pallas kernels: none -> 34.6 us  [the longest x4 18.9 us: local_part(): pl.pallas_call(functools.partial(local_kernel, part * count), out_shape=[...]
    all_to_all x3 -> x0, starting transfers between devices: 28.8 us -> none  [the longest x1 11.6 us: per_device(): lax.all_to_all(rows_decay, 'ctx', split_axis=0, concat_axis=1, tiled=True)]
    ppermute x0 -> x17, starting transfers between devices: none -> 26.2 us  [the longest x13 17.5 us: swap(): return lax.ppermute(a, 'ctx', [(i, i ^ mask) for i in range(ctx_size)])]
    dot_general x34 -> x0, matrix products: 21.9 us -> none  [the longest x32 11.7 us: block_local(): jnp.dot(probs, v_block[:, first_col:last_col], preferred_element_type=jnp...]
    all_to_all x3 -> x0, waiting for transfers between devices: 16.4 us -> none  [the longest x1 16.4 us: per_device(): lax.all_to_all(rows_state, 'ctx', split_axis=0, concat_axis=1, tiled=True)]
    unnamed x9 -> x12, local copies, waits for them, and re-layouts: 19.7 us -> 3.96 us
    ppermute x0 -> x17, waiting for transfers between devices: none -> 13.4 us  [the longest x13 11.6 us: swap(): return lax.ppermute(a, 'ctx', [(i, i ^ mask) for i in range(ctx_size)])]
  transfers between devices with their start and end apart: 4 -> 17, of which waited for: 2 -> 5; matrix products, arithmetic and copies ran while one was open for 30% -> 3% of each run, Pallas kernels for 0% -> 29%
where the time goes in v1:
time: 83.1 us; the launch traced here: 82.3 us
  Pallas kernels  34.6 us (42%)
  starting transfers between devices  26.2 us (32%)
  waiting for transfers between devices  13.4 us (16%)
  local copies, waits for them, and re-layouts  4.06 us (5%)
  other arithmetic  2.54 us (3%)
  between operations  1.51 us (2%)
    pallas_call x4, Pallas kernels, local_part(): pl.pallas_call(functools.partial(local_kernel, part * count), out_shape=[...  18.9 us
    ppermute x13, starting transfers between devices, swap(): return lax.ppermute(a, 'ctx', [(i, i ^ mask) for i in range(ctx_size)])  17.5 us
    ppermute x13, waiting for transfers between devices, swap(): return lax.ppermute(a, 'ctx', [(i, i ^ mask) for i in range(ctx_size)])  11.6 us
    ppermute x4, starting transfers between devices, swap_y(): return lax.ppermute(a, 'head', [(i, i ^ mask) for i in range(head_size)])  8.73 us
    pallas_call x2, Pallas kernels, summary(): pl.pallas_call(functools.partial(summary_kernel, first), out_shape=jax.Sh...  5.72 us
    pallas_call x1, Pallas kernels, last_part(): pl.pallas_call(functools.partial(last_kernel, count), out_shape=jax.Shape...  5.71 us
    pallas_call x7, Pallas kernels, call(): pl.pallas_call(kernel, out_shape=[jax.ShapeDtypeStruct(s, f32) for s in o...  4.24 us
    unnamed x12, local copies, waits for them, and re-layouts  3.96 us
  transfers between devices with their start and end apart: 17, of which 5 were waited for; matrix products, arithmetic and copies ran while one was open for 3% of the time, Pallas kernels for 29%

profile of v1, /device:TPU:32, one launch (start us, length us, event | category | flops | bytes accessed | tf_op | source)
XLA Modules:
  0.0 82.3 jit_solution(13090598864914501073)
XLA Ops:
  0.8 1.6 %copy-done = bf16[1024,1024]{1,0:T(8,128)(2,1)S(1)} copy-done((bf16[1024,1024]{1,0:T(8,128)(2,1)S(1)}, bf16[1024,1024]{1,0:T(8,128)(2,1)}, u32[]{:S(2)}) %copy-start) | copy-done | bytes 2097176
  2.4 1.6 %copy-done.2 = bf16[1024,1024]{1,0:T(8,128)(2,1)S(1)} copy-done((bf16[1024,1024]{1,0:T(8,128)(2,1)S(1)}, bf16[1024,1024]{1,0:T(8,128)(2,1)}, u32[]{:S(2)}) %copy-start.2) | copy-done | bytes 2097176
  3.9 0.8 copy-done.4
  4.7 2.9 %summary_a.1 = f32[4,136,128]{2,1,0:T(8,128)S(1)} custom-call(s32[6]{0:T(128)S(1)} %stack.27.idx_ref, bf16[1024,1024]{1,0:T(8,128)(2,1)S(1)} %copy-done, bf16[1024,1024]{1,0:T(8,128)(2,1)S(1)} %copy-done.2, f32[8,1024]{1,0:T(8,128)S(1)} %copy-done.4), custom_call_target="tpu_custom_call" | custom-call | flops 268435456 | bytes 2097152 | tf_op jit(solution)/shard_map/summary_a/pallas_call | solution.py:89
  7.7 2.9 %summary_b.1.keep_ref = f32[4,136,128]{2,1,0:T(8,128)S(1)} custom-call(s32[6]{0:T(128)S(1)} %stack.27.idx_ref, bf16[1024,1024]{1,0:T(8,128)(2,1)S(1)} %copy-done, bf16[1024,1024]{1,0:T(8,128)(2,1)S(1)} %copy-done.2, f32[8,1024]{1,0:T(8,128)S(1)} %copy-done.4), custom_call_target="tpu_custom_call" | custom-call | flops 268435456 | bytes 2097152 | tf_op jit(solution)/shard_map/summary_b/pallas_call | solution.py:89
  10.6 0.6 pair.1
  11.2 1.6 %collective-permute-start.4 = (f32[136,128]{1,0:T(8,128)S(1)}, f32[136,128]{1,0:T(8,128)S(1)}, u32[]{:S(2)}, u32[]{:S(2)}) collective-permute-start(f32[136,128]{1,0:T(8,128)S(1)} %get-tuple-element.27), channel_id=1, source_target_pairs={{0,8},{4,12},{8,0},{12,4},{16,24},{20,28},{24,16},{28,20},{32,40},... | collective-permute-start | bytes 208904 | tf_op jit(solution)/shard_map/ppermute | solution.py:344
  12.8 2.7 %collective-permute-start.5 = (f32[136,128]{1,0:T(8,128)S(1)}, f32[136,128]{1,0:T(8,128)S(1)}, u32[]{:S(2)}, u32[]{:S(2)}) collective-permute-start(f32[136,128]{1,0:T(8,128)S(1)} %get-tuple-element.28), channel_id=1, source_target_pairs={{0,16},{4,20},{8,24},{12,28},{16,0},{20,4},{24,8},{28,12},{32,48},... | collective-permute-start | bytes 208904 | tf_op jit(solution)/shard_map/ppermute | solution.py:344
  16.0 3.6 %collective-permute-done.5.t2 = f32[136,128]{1,0:T(8,128)S(1)} collective-permute-done((f32[136,128]{1,0:T(8,128)S(1)}, f32[136,128]{1,0:T(8,128)S(1)}, u32[]{:S(2)}, u32[]{:S(2)}) %collective-permute-start.5) | collective-permute-done | bytes 69664 | tf_op jit(solution)/shard_map/ppermute | solution.py:344
  19.6 1.5 %collective-permute-done.6.t3 = f32[136,128]{1,0:T(8,128)S(1)} collective-permute-done((f32[136,128]{1,0:T(8,128)S(1)}, f32[136,128]{1,0:T(8,128)S(1)}, u32[]{:S(2)}, u32[]{:S(2)}) %collective-permute-start.6) | collective-permute-done | bytes 69664 | tf_op jit(solution)/shard_map/ppermute | solution.py:344
  21.8 4.2 %collective-permute-done.7.r_ref = f32[136,128]{1,0:T(8,128)S(1)} collective-permute-done((f32[136,128]{1,0:T(8,128)S(1)}, f32[136,128]{1,0:T(8,128)S(1)}, u32[]{:S(2)}, u32[]{:S(2)}) %collective-permute-start.7) | collective-permute-done | bytes 69664 | tf_op jit(solution)/shard_map/ppermute | solution.py:344
  26.6 3.4 %collective-permute-start.8 = (f32[136,128]{1,0:T(8,128)S(1)}, f32[136,128]{1,0:T(8,128)S(1)}, u32[]{:S(2)}, u32[]{:S(2)}) collective-permute-start(f32[136,128]{1,0:T(8,128)S(1)} %get-tuple-element.30.g_ref), channel_id=1, source_target_pairs={{0,64},{4,68},{8,72},{12,76},{16,80},{20,84},{24,88},{28,92},{32,9... | collective-permute-start | bytes 208904 | tf_op jit(solution)/shard_map/ppermute | solution.py:344
  30.6 4.5 %local_attn.4 = (f32[1024,256]{1,0:T(8,128)S(1)}, f32[1024,8]{1,0:T(8,128)S(1)}) custom-call(bf16[1024,1024]{1,0:T(8,128)(2,1)S(1)} %copy-done.3, bf16[1024,1024]{1,0:T(8,128)(2,1)S(1)} %copy-done.1, bf16[1024,1024]{1,0:T(8,128)(2,1)S(1)} %copy-done.2, f32[8,1024]{1,0:T(8,128)S(1)} %copy-done.4), custom_call_target="tpu_custom_call" | custom-call | flops 402653184 | bytes 2621440 | tf_op jit(solution)/shard_map/local_attn/pallas_call | solution.py:277
  35.8 3.7 %collective-permute-start.9 = (f32[136,128]{1,0:T(8,128)S(1)}, f32[136,128]{1,0:T(8,128)S(1)}, u32[]{:S(2)}, u32[]{:S(2)}) collective-permute-start(f32[136,128]{1,0:T(8,128)S(1)} %get-tuple-element.32.g_ref), channel_id=1, source_target_pairs={{0,192},{4,196},{8,200},{12,204},{16,208},{20,212},{24,216},{28,22... | collective-permute-start | bytes 208904 | tf_op jit(solution)/shard_map/ppermute | solution.py:344
  39.4 0.6 pad_add_fusion
  40.1 1.6 %collective-permute-start.1 = (s32[2]{0:T(128)S(1)}, s32[2]{0:T(128)S(1)}, u32[]{:S(2)}, u32[]{:S(2)}) collective-permute-start(s32[2]{0:T(128)S(1)} %pad_add_fusion), channel_id=1, source_target_pairs={{0,1},{1,0},{2,3},{3,2},{4,5},{5,4},{6,7},{7,6},{8,9},{9,8},{10,11... | collective-permute-start | bytes 32 | tf_op jit(solution)/shard_map/ppermute | solution.py:347
  41.7 2.4 %collective-permute-done.9.r_ref = f32[136,128]{1,0:T(8,128)S(1)} collective-permute-done((f32[136,128]{1,0:T(8,128)S(1)}, f32[136,128]{1,0:T(8,128)S(1)}, u32[]{:S(2)}, u32[]{:S(2)}) %collective-permute-start.9) | collective-permute-done | bytes 69664 | tf_op jit(solution)/shard_map/ppermute | solution.py:344
  44.6 0.6 back.1
  45.4 2.6 %collective-permute-start.11 = (f32[256,128]{1,0:T(8,128)S(1)}, f32[256,128]{1,0:T(8,128)S(1)}, u32[]{:S(2)}, u32[]{:S(2)}) collective-permute-start(f32[256,128]{1,0:T(8,128)S(1)} %get-tuple-element.38), channel_id=1, source_target_pairs={{0,16},{4,20},{8,24},{12,28},{16,0},{20,4},{24,8},{28,12},{32,48},... | collective-permute-start | bytes 393224 | tf_op jit(solution)/shard_map/ppermute | solution.py:344
  47.9 2.1 %collective-permute-start.12 = (f32[256,128]{1,0:T(8,128)S(1)}, f32[256,128]{1,0:T(8,128)S(1)}, u32[]{:S(2)}, u32[]{:S(2)}) collective-permute-start(f32[256,128]{1,0:T(8,128)S(1)} %get-tuple-element.39), channel_id=1, source_target_pairs={{0,24},{4,28},{8,16},{12,20},{16,8},{20,12},{24,0},{28,4},{32,56},... | collective-permute-start | bytes 393224 | tf_op jit(solution)/shard_map/ppermute | solution.py:344
  50.0 0.6 pad_add_fusion.1
  50.7 3.0 %collective-permute-start.2 = (s32[4]{0:T(128)S(1)}, s32[4]{0:T(128)S(1)}, u32[]{:S(2)}, u32[]{:S(2)}) collective-permute-start(s32[4]{0:T(128)S(1)} %pad_add_fusion.1), channel_id=1, source_target_pairs={{0,3},{1,2},{2,1},{3,0},{4,7},{5,6},{6,5},{7,4},{8,11},{9,10},{10,... | collective-permute-start | bytes 56 | tf_op jit(solution)/shard_map/ppermute | solution.py:347
  53.7 1.7 %collective-permute-done.2 = s32[4]{0:T(128)S(1)} collective-permute-done((s32[4]{0:T(128)S(1)}, s32[4]{0:T(128)S(1)}, u32[]{:S(2)}, u32[]{:S(2)}) %collective-permute-start.2) | collective-permute-done | bytes 48 | tf_op jit(solution)/shard_map/ppermute | solution.py:347
  55.5 0.6 pad_add_fusion.2.want_ref
  56.1 0.7 spread.1
  56.8 1.6 %collective-permute-start.14 = (f32[4,16,128]{2,1,0:T(8,128)S(1)}, f32[4,16,128]{2,1,0:T(8,128)S(1)}, u32[]{:S(2)}, u32[]{:S(2)}) collective-permute-start(f32[4,16,128]{2,1,0:T(8,128)S(1)} %get-tuple-element.47), channel_id=1, source_target_pairs={{0,1},{1,0},{2,3},{3,2},{4,5},{5,4},{6,7},{7,6},{8,9},{9,8},{10,11... | collective-permute-start | bytes 98312 | tf_op jit(solution)/shard_map/ppermute | solution.py:347
  58.5 4.8 %local_attn.6 = (f32[1024,256]{1,0:T(8,128)S(1)}, f32[1024,8]{1,0:T(8,128)}) custom-call(bf16[1024,1024]{1,0:T(8,128)(2,1)S(1)} %copy-done.3, bf16[1024,1024]{1,0:T(8,128)(2,1)S(1)} %copy-done.1, bf16[1024,1024]{1,0:T(8,128)(2,1)S(1)} %copy-done.2, f32[8,1024]{1,0:T(8,128)S(1)} %copy-done.4), custom_call_target="tpu_custom_call" | custom-call | flops 402653184 | bytes 2621440 | tf_op jit(solution)/shard_map/local_attn/pallas_call | solution.py:277
  63.3 2.5 %collective-permute-start.15 = (f32[2,16,128]{2,1,0:T(8,128)S(1)}, f32[2,16,128]{2,1,0:T(8,128)S(1)}, u32[]{:S(2)}, u32[]{:S(2)}) collective-permute-start(f32[2,16,128]{2,1,0:T(8,128)S(1)} %slice.17), channel_id=1, source_target_pairs={{0,3},{1,2},{2,1},{3,0},{4,7},{5,6},{6,5},{7,4},{8,11},{9,10},{10,... | collective-permute-start | bytes 49160 | tf_op jit(solution)/shard_map/ppermute | solution.py:347
  65.8 4.8 %local_attn.5 = (f32[1024,256]{1,0:T(8,128)S(1)}, f32[1024,8]{1,0:T(8,128)}) custom-call(bf16[1024,1024]{1,0:T(8,128)(2,1)S(1)} %copy-done.3, bf16[1024,1024]{1,0:T(8,128)(2,1)S(1)} %copy-done.1, bf16[1024,1024]{1,0:T(8,128)(2,1)S(1)} %copy-done.2, f32[8,1024]{1,0:T(8,128)S(1)} %copy-done.4), custom_call_target="tpu_custom_call" | custom-call | flops 402653184 | bytes 2621440 | tf_op jit(solution)/shard_map/local_attn/pallas_call | solution.py:277
  71.2 4.8 %local_attn.7 = (f32[1024,256]{1,0:T(8,128)S(1)}, f32[1024,8]{1,0:T(8,128)}) custom-call(bf16[1024,1024]{1,0:T(8,128)(2,1)S(1)} %copy-done.3, bf16[1024,1024]{1,0:T(8,128)(2,1)S(1)} %copy-done.1, bf16[1024,1024]{1,0:T(8,128)(2,1)S(1)} %copy-done.2, f32[8,1024]{1,0:T(8,128)S(1)} %copy-done.4), custom_call_target="tpu_custom_call" | custom-call | flops 402653184 | bytes 2621440 | tf_op jit(solution)/shard_map/local_attn/pallas_call | solution.py:277
  76.0 0.6 fusion
  76.6 5.7 %last.1 = bf16[1024,1024]{1,0:T(8,128)(2,1)} custom-call(s32[6]{0:T(128)S(1)} %stack.27.idx_ref, bf16[1024,1024]{1,0:T(8,128)(2,1)S(1)} %copy-done.3, f32[1024,8]{1,0:T(8,128)S(1)} %get-tuple-element.25.e_ref, f32[1,1024]{1,0:T(1,128)S(1)} %bitcast.13, f32[4,128,128]{2,1,0:T(8,128)S(1)} %get-tuple-element.40.own_ref, ...), custom_call_target="tpu_custom_call" | custom-call | flops 536870912 | bytes 8388608 | tf_op jit(solution)/shard_map/last/pallas_call | solution.py:318
  (38 shorter events, 3.9 us)
Async XLA Ops:
  0.8 1.6 %copy-start = (bf16[1024,1024]{1,0:T(8,128)(2,1)S(1)}, bf16[1024,1024]{1,0:T(8,128)(2,1)}, u32[]{:S(2)}) copy-start(bf16[1024,1024]{1,0:T(8,128)(2,1)} %k_ref.11) | copy-start | bytes 6291460
  2.4 1.6 %copy-start.2 = (bf16[1024,1024]{1,0:T(8,128)(2,1)S(1)}, bf16[1024,1024]{1,0:T(8,128)(2,1)}, u32[]{:S(2)}) copy-start(bf16[1024,1024]{1,0:T(8,128)(2,1)} %v_ref.11) | copy-start | bytes 6291460
  3.9 0.8 copy-start.4
  7.6 23.1 %copy-start.1 = (bf16[1024,1024]{1,0:T(8,128)(2,1)S(1)}, bf16[1024,1024]{1,0:T(8,128)(2,1)}, u32[]{:S(2)}) copy-start(bf16[1024,1024]{1,0:T(8,128)(2,1)} %k_ref.11) | copy-start | bytes 6291460
  7.6 23.1 %copy-start.3 = (bf16[1024,1024]{1,0:T(8,128)(2,1)S(1)}, bf16[1024,1024]{1,0:T(8,128)(2,1)}, u32[]{:S(2)}) copy-start(bf16[1024,1024]{1,0:T(8,128)(2,1)} %q_ref.9) | copy-start | bytes 6291460
  7.6 3.0 %collective-permute-start.3 = (f32[4,136,128]{2,1,0:T(8,128)S(1)}, f32[4,136,128]{2,1,0:T(8,128)S(1)}, u32[]{:S(2)}, u32[]{:S(2)}) collective-permute-start(f32[4,136,128]{2,1,0:T(8,128)S(1)} %summary_a.1), channel_id=1, source_target_pairs={{0,4},{4,0},{8,12},{12,8},{16,20},{20,16},{24,28},{28,24},{32,36},... | collective-permute-start | bytes 835592 | tf_op jit(solution)/shard_map/ppermute | solution.py:344
  11.2 4.8 %collective-permute-start.4 = (f32[136,128]{1,0:T(8,128)S(1)}, f32[136,128]{1,0:T(8,128)S(1)}, u32[]{:S(2)}, u32[]{:S(2)}) collective-permute-start(f32[136,128]{1,0:T(8,128)S(1)} %get-tuple-element.27), channel_id=1, source_target_pairs={{0,8},{4,12},{8,0},{12,4},{16,24},{20,28},{24,16},{28,20},{32,40},... | collective-permute-start | bytes 208904 | tf_op jit(solution)/shard_map/ppermute | solution.py:344
  12.8 6.8 %collective-permute-start.5 = (f32[136,128]{1,0:T(8,128)S(1)}, f32[136,128]{1,0:T(8,128)S(1)}, u32[]{:S(2)}, u32[]{:S(2)}) collective-permute-start(f32[136,128]{1,0:T(8,128)S(1)} %get-tuple-element.28), channel_id=1, source_target_pairs={{0,16},{4,20},{8,24},{12,28},{16,0},{20,4},{24,8},{28,12},{32,48},... | collective-permute-start | bytes 208904 | tf_op jit(solution)/shard_map/ppermute | solution.py:344
  15.5 5.5 %collective-permute-start.6 = (f32[136,128]{1,0:T(8,128)S(1)}, f32[136,128]{1,0:T(8,128)S(1)}, u32[]{:S(2)}, u32[]{:S(2)}) collective-permute-start(f32[136,128]{1,0:T(8,128)S(1)} %get-tuple-element.29), channel_id=1, source_target_pairs={{0,24},{4,28},{8,16},{12,20},{16,8},{20,12},{24,0},{28,4},{32,56},... | collective-permute-start | bytes 208904 | tf_op jit(solution)/shard_map/ppermute | solution.py:344
  21.6 4.4 %collective-permute-start.7 = (f32[136,128]{1,0:T(8,128)S(1)}, f32[136,128]{1,0:T(8,128)S(1)}, u32[]{:S(2)}, u32[]{:S(2)}) collective-permute-start(f32[136,128]{1,0:T(8,128)S(1)} %slab.1.g_ref), channel_id=1, source_target_pairs={{0,32},{4,36},{8,40},{12,44},{16,48},{20,52},{24,56},{28,60},{32,0... | collective-permute-start | bytes 208904 | tf_op jit(solution)/shard_map/ppermute | solution.py:344
  26.6 8.6 %collective-permute-start.8 = (f32[136,128]{1,0:T(8,128)S(1)}, f32[136,128]{1,0:T(8,128)S(1)}, u32[]{:S(2)}, u32[]{:S(2)}) collective-permute-start(f32[136,128]{1,0:T(8,128)S(1)} %get-tuple-element.30.g_ref), channel_id=1, source_target_pairs={{0,64},{4,68},{8,72},{12,76},{16,80},{20,84},{24,88},{28,92},{32,9... | collective-permute-start | bytes 208904 | tf_op jit(solution)/shard_map/ppermute | solution.py:344
  30.0 9.5 %collective-permute-start = (s32[1]{0:T(128)}, s32[1]{0:T(128)}, u32[]{:S(2)}, u32[]{:S(2)}) collective-permute-start(s32[1]{0:T(128)} %param.11), channel_id=1, source_target_pairs={{0,4},{4,0},{8,12},{12,8},{16,20},{20,16},{24,28},{28,24},{32,36},... | collective-permute-start | bytes 20 | tf_op jit(solution)/shard_map/ppermute | solution.py:344
  35.8 8.3 %collective-permute-start.9 = (f32[136,128]{1,0:T(8,128)S(1)}, f32[136,128]{1,0:T(8,128)S(1)}, u32[]{:S(2)}, u32[]{:S(2)}) collective-permute-start(f32[136,128]{1,0:T(8,128)S(1)} %get-tuple-element.32.g_ref), channel_id=1, source_target_pairs={{0,192},{4,196},{8,200},{12,204},{16,208},{20,212},{24,216},{28,22... | collective-permute-start | bytes 208904 | tf_op jit(solution)/shard_map/ppermute | solution.py:344
  40.1 10.0 %collective-permute-start.1 = (s32[2]{0:T(128)S(1)}, s32[2]{0:T(128)S(1)}, u32[]{:S(2)}, u32[]{:S(2)}) collective-permute-start(s32[2]{0:T(128)S(1)} %pad_add_fusion), channel_id=1, source_target_pairs={{0,1},{1,0},{2,3},{3,2},{4,5},{5,4},{6,7},{7,6},{8,9},{9,8},{10,11... | collective-permute-start | bytes 32 | tf_op jit(solution)/shard_map/ppermute | solution.py:347
  45.3 10.9 %collective-permute-start.10 = (f32[256,128]{1,0:T(8,128)S(1)}, f32[256,128]{1,0:T(8,128)S(1)}, u32[]{:S(2)}, u32[]{:S(2)}) collective-permute-start(f32[256,128]{1,0:T(8,128)S(1)} %get-tuple-element.37), channel_id=1, source_target_pairs={{0,8},{4,12},{8,0},{12,4},{16,24},{20,28},{24,16},{28,20},{32,40},... | collective-permute-start | bytes 393224 | tf_op jit(solution)/shard_map/ppermute | solution.py:344
  45.4 10.8 %collective-permute-start.11 = (f32[256,128]{1,0:T(8,128)S(1)}, f32[256,128]{1,0:T(8,128)S(1)}, u32[]{:S(2)}, u32[]{:S(2)}) collective-permute-start(f32[256,128]{1,0:T(8,128)S(1)} %get-tuple-element.38), channel_id=1, source_target_pairs={{0,16},{4,20},{8,24},{12,28},{16,0},{20,4},{24,8},{28,12},{32,48},... | collective-permute-start | bytes 393224 | tf_op jit(solution)/shard_map/ppermute | solution.py:344
  47.9 8.2 %collective-permute-start.12 = (f32[256,128]{1,0:T(8,128)S(1)}, f32[256,128]{1,0:T(8,128)S(1)}, u32[]{:S(2)}, u32[]{:S(2)}) collective-permute-start(f32[256,128]{1,0:T(8,128)S(1)} %get-tuple-element.39), channel_id=1, source_target_pairs={{0,24},{4,28},{8,16},{12,20},{16,8},{20,12},{24,0},{28,4},{32,56},... | collective-permute-start | bytes 393224 | tf_op jit(solution)/shard_map/ppermute | solution.py:344
  50.7 4.8 %collective-permute-start.2 = (s32[4]{0:T(128)S(1)}, s32[4]{0:T(128)S(1)}, u32[]{:S(2)}, u32[]{:S(2)}) collective-permute-start(s32[4]{0:T(128)S(1)} %pad_add_fusion.1), channel_id=1, source_target_pairs={{0,3},{1,2},{2,1},{3,0},{4,7},{5,6},{6,5},{7,4},{8,11},{9,10},{10,... | collective-permute-start | bytes 56 | tf_op jit(solution)/shard_map/ppermute | solution.py:347
  56.8 6.4 %collective-permute-start.14 = (f32[4,16,128]{2,1,0:T(8,128)S(1)}, f32[4,16,128]{2,1,0:T(8,128)S(1)}, u32[]{:S(2)}, u32[]{:S(2)}) collective-permute-start(f32[4,16,128]{2,1,0:T(8,128)S(1)} %get-tuple-element.47), channel_id=1, source_target_pairs={{0,1},{1,0},{2,3},{3,2},{4,5},{5,4},{6,7},{7,6},{8,9},{9,8},{10,11... | collective-permute-start | bytes 98312 | tf_op jit(solution)/shard_map/ppermute | solution.py:347
  63.3 7.3 %collective-permute-start.15 = (f32[2,16,128]{2,1,0:T(8,128)S(1)}, f32[2,16,128]{2,1,0:T(8,128)S(1)}, u32[]{:S(2)}, u32[]{:S(2)}) collective-permute-start(f32[2,16,128]{2,1,0:T(8,128)S(1)} %slice.17), channel_id=1, source_target_pairs={{0,3},{1,2},{2,1},{3,0},{4,7},{5,6},{6,5},{7,4},{8,11},{9,10},{10,... | collective-permute-start | bytes 49160 | tf_op jit(solution)/shard_map/ppermute | solution.py:347
  70.6 6.0 %collective-permute-start.13 = (f32[4,128,128]{2,1,0:T(8,128)S(1)}, f32[4,128,128]{2,1,0:T(8,128)S(1)}, u32[]{:S(2)}, u32[]{:S(2)}) collective-permute-start(f32[4,128,128]{2,1,0:T(8,128)S(1)} %get-tuple-element.41), channel_id=1, source_target_pairs={{0,4},{4,0},{8,12},{12,8},{16,20},{20,16},{24,28},{28,24},{32,36},... | collective-permute-start | bytes 786440 | tf_op jit(solution)/shard_map/ppermute | solution.py:344
  70.6 6.0 %copy-start.5 = (f32[1024]{0:T(1024)S(1)}, f32[1024]{0:T(1024)}, u32[]{:S(2)}) copy-start(f32[1024]{0:T(1024)} %param.10) | copy-start | bytes 12292
  70.6 5.4 %collective-permute-start.16 = (f32[16,128]{1,0:T(8,128)S(1)}, f32[16,128]{1,0:T(8,128)S(1)}, u32[]{:S(2)}, u32[]{:S(2)}) collective-permute-start(f32[16,128]{1,0:T(8,128)S(1)} %slice_bitcast_fusion), channel_id=1, source_target_pairs={{0,4},{4,0},{8,12},{12,8},{16,20},{20,16},{24,28},{28,24},{32,36},... | collective-permute-start | bytes 24584 | tf_op jit(solution)/shard_map/ppermute | solution.py:344

commit v2 on v0

v2 whole, which is shorter than its diff:
```python
import functools

import jax
import jax.numpy as jnp
from jax import lax
from jax.experimental import pallas as pl
from jax.experimental.pallas import tpu as pltpu
from jax.sharding import PartitionSpec as P

BLK = 256
EXT = 8
f32 = jnp.float32
bf16 = jnp.bfloat16
SMEM = pl.BlockSpec(memory_space=pltpu.SMEM)
VMEM = pl.BlockSpec(memory_space=pltpu.VMEM)
HBM = pl.BlockSpec(memory_space=pltpu.HBM)
ANY = pl.BlockSpec(memory_space=pl.ANY)
FAR_FIRST = (0, 2, 1, 3)
LOG2E = 1.4426950408889634
PARAMS = pltpu.CompilerParams(vmem_limit_bytes=40 * 1024 * 1024)


def dot(a, b):
    return lax.dot_general(a, b, (((1,), (0,)), ((), ())), preferred_element_type=f32)


def split2(x):
    hi = x.astype(bf16)
    return hi, (x - hi.astype(f32)).astype(bf16)


def split3(x):
    hi = x.astype(bf16)
    rest = x - hi.astype(f32)
    mid = rest.astype(bf16)
    return hi, mid, (rest - mid.astype(f32)).astype(bf16)


def block_cums(ld):
    heads, tokens = ld.shape
    n = tokens // BLK
    row = lax.broadcasted_iota(jnp.int32, (BLK, BLK), 0)
    col = lax.broadcasted_iota(jnp.int32, (BLK, BLK), 1)
    tri = jnp.where(row <= col, 1.0, 0.0).astype(bf16)
    parts = []
    for j in range(n):
        parts += list(split3(ld[:, j * BLK : (j + 1) * BLK].astype(f32)))
    stacked = jnp.concatenate([p.astype(f32) for p in parts], axis=0).astype(bf16)
    sums = dot(stacked, tri)
    out = []
    for j in range(n):
        a = sums[(3 * j) * heads : (3 * j + 1) * heads]
        b = sums[(3 * j + 1) * heads : (3 * j + 2) * heads]
        c = sums[(3 * j + 2) * heads : (3 * j + 3) * heads]
        out.append(a + (b + c))
    return out


def place():
    at = lax.axis_index("ctx")
    return at & 1, (at >> 1) & 3, at >> 3, lax.axis_index("head")


def kept_first(ld, core):
    half = ld.shape[0] // 2
    return jnp.where(core == 0, ld, jnp.concatenate([ld[half:], ld[:half]], axis=0))


def state_sum(k, v, w):
    kt = k.T.astype(f32) * w
    hi, lo = split2(kt)
    both = dot(jnp.concatenate([hi, lo], axis=0), v)
    return both[:128] + both[128:]


def write_sum(s_ref, i, state, tot_ref, h):
    s_ref[i, 0:128, :] = state
    heads = tot_ref.shape[0] - 8
    s_ref[i, 128:135, :] = jnp.broadcast_to(tot_ref[h : h + 1, :], (7, 128))
    s_ref[i, 135:136, :] = tot_ref[heads : heads + 1, :]


def send_kernel(k_hbm, v_hbm, ld_hbm, map_ref, s_ref, w_ref, tot_ref, k_ref, v_ref, ld_buf, sems, ld_sem):
    core = place()[0]
    heads, tokens = ld_buf.shape
    half = heads // 2
    ld_copy = pltpu.make_async_copy(ld_hbm, ld_buf, ld_sem)
    ld_copy.start()
    copies = {}

    def fetch(i):
        col = pl.multiple_of(((i + half * core) % heads) * 128, 128)
        copies[i] = [
            pltpu.make_async_copy(src.at[:, pl.ds(col, 128)], buf.at[i], sems.at[n, i])
            for n, (src, buf) in enumerate(((k_hbm, k_ref), (v_hbm, v_ref)))
        ]
        for copy in copies[i]:
            copy.start()

    for i in range(half, heads):
        fetch(i)
    ld_copy.wait()
    for i in range(half):
        fetch(i)
    ld = kept_first(ld_buf[...], core)
    n = tokens // BLK
    cums = block_cums(ld)
    after = jnp.zeros((heads, 1), f32)
    for j in reversed(range(n)):
        total = cums[j][:, BLK - 1 : BLK]
        w_ref[:, j * BLK : (j + 1) * BLK] = jnp.exp(total - cums[j] + after)
        after = after + total
    tot_ref[0:heads, :] = jnp.broadcast_to(after, (heads, 128))
    tot_ref[heads:, :] = jnp.full((8, 128), map_ref[0], jnp.int32).astype(f32)
    for i in range(half):
        h = i + half
        for copy in copies[h]:
            copy.wait()
        write_sum(s_ref, i, state_sum(k_ref[h], v_ref[h], w_ref[h : h + 1, :]), tot_ref, h)
    for i in range(half):
        for copy in copies[i]:
            copy.wait()


def keep_kernel(k_ref, v_ref, w_ref, tot_ref, s_ref):
    for i in range(s_ref.shape[0]):
        write_sum(s_ref, i, state_sum(k_ref[i], v_ref[i], w_ref[i : i + 1, :]), tot_ref, i)


def summaries(keys, values, ld, decode_map):
    tokens, _ = keys.shape
    heads = ld.shape[0]
    half = heads // 2
    out = jax.ShapeDtypeStruct((half, 128 + EXT, 128), f32)
    by_head = jax.ShapeDtypeStruct((heads, tokens, 128), bf16)
    cost = pl.CostEstimate(flops=2 * 2 * half * tokens * 128 * 128, bytes_accessed=2 * tokens * heads * 128, transcendentals=0)
    inputs = [pltpu.with_memory_space_constraint(a, pltpu.HBM) for a in (keys, values, ld)]
    send, w, tot, k_heads, v_heads = pl.pallas_call(
        send_kernel,
        out_shape=[
            out,
            jax.ShapeDtypeStruct((heads, tokens), f32),
            jax.ShapeDtypeStruct((heads + 8, 128), f32),
            by_head,
            by_head,
        ],
        in_specs=[HBM, HBM, HBM, SMEM],
        out_specs=[VMEM] * 5,
        scratch_shapes=[
            pltpu.VMEM((heads, tokens), f32),
            pltpu.SemaphoreType.DMA((2, heads)),
            pltpu.SemaphoreType.DMA(()),
        ],
        compiler_params=PARAMS,
        cost_estimate=cost,
        name="summary_send",
    )(*inputs, decode_map)
    keep = pl.pallas_call(
        keep_kernel,
        out_shape=out,
        in_specs=[VMEM] * 4,
        out_specs=VMEM,
        compiler_params=PARAMS,
        cost_estimate=cost,
        name="summary_keep",
    )(k_heads, v_heads, w, tot)
    return send, keep, k_heads, v_heads


def compose(early, late):
    scale = jnp.exp(late[1])
    return (scale[0:1] * early[0] + late[0], early[1] + late[1])


def parts(ref):
    return (ref[0:128, :], ref[128:136, :])


def pair_kernel(keep_ref, recv_ref, *outs):
    core, x, _, _ = place()
    zero = core == 0
    for n, d in enumerate(FAR_FIRST):
        j = x ^ d
        own = (keep_ref[j, 0:128, :], keep_ref[j, 128:136, :])
        got = (recv_ref[j, 0:128, :], recv_ref[j, 128:136, :])
        early = tuple(jnp.where(zero, a, b) for a, b in zip(own, got))
        late = tuple(jnp.where(zero, b, a) for a, b in zip(own, got))
        state, decay = compose(early, late)
        outs[n][0:128, :] = state
        outs[n][128:136, :] = decay
    outs[4][0:1, :] = keep_ref[0, 135:136, :]
    outs[4][1:2, :] = recv_ref[0, 135:136, :]
    outs[4][2:8, :] = jnp.zeros((6, 128), f32)


def pick(x, j, refs):
    state, decay = parts(refs[0])
    for n in range(1, 4):
        here = (x ^ FAR_FIRST[n]) == j
        s, e = parts(refs[n])
        state, decay = jnp.where(here, s, state), jnp.where(here, e, decay)
    return state, decay


def slab_kernel(t0, t1, t2, t3, u_ref):
    _, x, _, _ = place()
    refs = (t0, t1, t2, t3)
    total = pick(x, 0, refs)
    for j in range(1, 4):
        total = compose(total, pick(x, j, refs))
    u_ref[0:128, :] = total[0]
    u_ref[128:136, :] = total[1]


def want_kernel(want_ref, got_ref, w_ref):
    w_ref[0:2, :] = want_ref[0:2, :]
    w_ref[2:4, :] = got_ref[0:2, :]
    w_ref[4:8, :] = jnp.zeros((4, 128), f32)


def round_kernel(bit, g_ref, r_ref, *rest):
    a_ref = rest[0] if len(rest) == 3 else None
    g_out, a_out = rest[-2:]
    late = ((place()[2] >> bit) & 1) == 1
    g, r = parts(g_ref), parts(r_ref)
    early_part = tuple(jnp.where(late, p, q) for p, q in zip(r, g))
    late_part = tuple(jnp.where(late, p, q) for p, q in zip(g, r))
    state, decay = compose(early_part, late_part)
    g_out[0:128, :] = state
    g_out[128:136, :] = decay
    a = parts(a_ref) if a_ref is not None else tuple(jnp.zeros_like(p) for p in r)
    state, decay = compose(r, a)
    a_out[0:128, :] = jnp.where(late, state, a[0])
    a_out[128:136, :] = jnp.where(late, decay, a[1])


def back_kernel(g_ref, a_ref, t0, t1, t2, t3, *outs):
    _, x, _, _ = place()
    refs = (t0, t1, t2, t3)
    before = [parts(a_ref)]
    for j in range(3):
        before.append(compose(before[-1], pick(x, j, refs)))
    for n, d in enumerate(FAR_FIRST):
        j = x ^ d
        state = before[0][0]
        for i in range(1, 4):
            state = jnp.where(j == i, before[i][0], state)
        outs[n][0:128, :] = state
        outs[n][128:256, :] = g_ref[0:128, :]


def spread_kernel(want_a, want_b, m0, m1, m2, m3, keep_ref, recv_ref, own_ref, send_ref, slot_ref):
    core, x, _, y = place()
    zero = core == 0
    refs = (m0, m1, m2, m3)
    for n, d in enumerate(FAR_FIRST):
        j = x ^ d
        chip = refs[n][0:128, :]
        s0 = jnp.where(zero, keep_ref[j, 0:128, :], recv_ref[j, 0:128, :])
        l0 = jnp.where(zero, keep_ref[j, 128:129, :], recv_ref[j, 128:129, :])
        second = jnp.exp(l0) * chip + s0
        own_ref[j] = jnp.where(zero, chip, second)
        send_ref[j, 0:128, :] = jnp.where(zero, second, chip)
    base = (y * 2 + core) * 32
    for slot in range(8):
        away = (0, 1, 3, 2)[slot // 2]
        want = (want_a if slot < 4 else want_b)[slot % 4 : slot % 4 + 1, :]
        rows = jnp.zeros((16, 128), f32)
        for n, d in enumerate(FAR_FIRST):
            for r in range(8):
                number = (base + (x ^ d) * 8 + r).astype(f32)
                rows = jnp.where(want == number, refs[n][128 + r * 16 : 144 + r * 16, :], rows)
        if slot % 2:
            send_ref[away, 128:144, :] = rows
        else:
            slot_ref[away] = rows


def merge_kernel(slot_ref, got_ref, send_ref, near_ref, far_ref):
    both = [slot_ref[d] + got_ref[d, 128:144, :] for d in range(4)]
    near_ref[...], far_ref[...] = both[0], both[3]
    send_ref[0], send_ref[1] = both[1], both[2]


def slots_kernel(got_ref, a_ref, b_ref, near_ref, far_ref):
    near_ref[...] = a_ref[...] + got_ref[0]
    far_ref[...] = b_ref[...] + got_ref[1]


def add_kernel(a_ref, b_ref, out_ref):
    out_ref[...] = a_ref[...] + b_ref[...]


def small(kernel, outs, name, after=()):
    def call(*args):
        def body(*refs):
            kernel(*refs[: len(args)], *refs[len(args) + len(after) :])

        return pl.pallas_call(
            body,
            out_shape=[jax.ShapeDtypeStruct(s, f32) for s in outs],
            in_specs=[VMEM] * len(args) + [ANY] * len(after),
            out_specs=[VMEM] * len(outs),
            compiler_params=PARAMS,
            name=name,
        )(*args, *after)

    return call


def prep_kernel(ld_ref, cr_ref, ct_ref):
    core = place()[0]
    ld = kept_first(ld_ref[...], core)
    for j, cum in enumerate(block_cums(ld)):
        rows = slice(j * BLK, (j + 1) * BLK)
        cum = cum * LOG2E
        cr_ref[:, rows] = cum
        ct_ref[rows, :] = cum.T


def local_kernel(heads, q_ref, k_ref, v_ref, cr_ref, ct_ref, *rest):
    core = place()[0]
    total_heads, tokens = cr_ref.shape
    outs, scaled = rest[: len(heads)], rest[len(heads) :]
    h2 = BLK // 2
    row = lax.broadcasted_iota(jnp.int32, (h2, h2), 0)
    col = lax.broadcasted_iota(jnp.int32, (h2, h2), 1)
    causal = row >= col
    for i, out, qs in zip(heads, outs, scaled):
        at = pl.multiple_of(((i + total_heads // 2 * core) % total_heads) * 128, 128)
        run = None
        off = jnp.zeros((1, 1), f32)
        for j in range(tokens // BLK):
            rows = slice(j * BLK, (j + 1) * BLK)
            q, k, v = q_ref[rows, pl.ds(at, 128)], k_ref[i, rows, :], v_ref[i, rows, :]
            c_row = cr_ref[i : i + 1, rows]
            c_col = ct_ref[rows, i : i + 1]
            total = c_row[:, BLK - 1 : BLK]
            decay = jnp.broadcast_to(jnp.exp2(c_col), (BLK, 128))
            hi, lo = split2(q.astype(f32) * (decay * jnp.exp2(off)))
            qs[rows, 0:128] = hi
            qs[rows, 128:256] = lo
            off = off + total
            for t in range(2):
                part = slice(t * h2, (t + 1) * h2)
                seen = (t + 1) * h2
                scores = lax.dot_general(q[part], k[:seen], (((1,), (1,)), ((), ())), preferred_element_type=f32)
                gap = c_col[part] - c_row[:, :seen]
                inner = jnp.where(causal, jnp.exp2(jnp.where(causal, gap[:, t * h2 :], 0.0)), 0.0)
                weights = inner if t == 0 else jnp.concatenate([jnp.exp2(gap[:, :h2]), inner], axis=1)
                attn = dot((scores * weights).astype(bf16), v[:seen])
                if run is not None:
                    twice = jnp.concatenate([q[part], q[part]], axis=1)
                    attn = attn + dot(twice, halves) * decay[part]
                out[j * BLK + t * h2 : j * BLK + seen, :] = attn
            if j + 1 < tokens // BLK:
                new = state_sum(k, v, jnp.exp2(total - c_row))
                run = new if run is None else run * jnp.exp2(total) + new
                halves = jnp.concatenate(split2(run), axis=0)


def local_part(heads, queries, keys, values, cr, ct, after):
    tokens = queries.shape[0]
    n = len(heads)

    def body(*refs):
        local_kernel(heads, *refs[:5], *refs[5 + len(after) :])

    return pl.pallas_call(
        body,
        out_shape=[jax.ShapeDtypeStruct((tokens, 128), f32)] * n + [jax.ShapeDtypeStruct((tokens, 256), bf16)] * n,
        in_specs=[VMEM] * 5 + [ANY] * len(after),
        out_specs=[VMEM] * 2 * n,
        compiler_params=PARAMS,
        cost_estimate=pl.CostEstimate(flops=n * tokens * 2 * 128 * (256 + 256 + 256), bytes_accessed=10 * tokens * 128 * n, transcendentals=n * tokens * 200),
        name="local_attn",
    )(queries, keys, values, cr, ct, *after)


def last_kernel(heads, gain_ref, p_ref, *rest):
    half, n = p_ref.shape[0], len(heads)
    attn_refs, q_refs = rest[:n], rest[n : 2 * n]
    out_ref, mark_ref, buf, sems = rest[-4:]
    mark_ref[...] = jnp.zeros(mark_ref.shape, f32)
    first = pl.multiple_of(((heads[0] + half * place()[0]) % (2 * half)) * 128, 128 * n)
    tokens = buf.shape[0]
    state = []
    for i in heads:
        hi, lo = split2(p_ref[i % half, 0:128, :])
        state.append((jnp.concatenate([hi, hi], axis=0), lo))
    copies = []
    for j in range(tokens // BLK):
        rows = slice(j * BLK, (j + 1) * BLK)
        for i in range(n):
            at = pl.multiple_of(first + i * 128, 128)
            both = q_refs[i][rows, :]
            carried = dot(both, state[i][0]) + dot(both[:, :128], state[i][1])
            attn = attn_refs[i][rows, :] + carried
            mean = jnp.mean(attn * attn, axis=1, keepdims=True)
            normed = attn * lax.rsqrt(mean + 1e-5) * gain_ref[:, pl.ds(at, 128)]
            buf[rows, i * 128 : (i + 1) * 128] = normed.astype(bf16)
        copy = pltpu.make_async_copy(buf.at[rows, :], out_ref.at[rows, pl.ds(first, n * 128)], sems.at[j])
        copy.start()
        copies.append(copy)
    for copy in copies:
        copy.wait()


def last_part(heads, gain, state, attn, scaled, out=None, after=()):
    n = len(heads)
    tokens, width = attn[0].shape[0], gain.shape[1]
    given = ([] if out is None else [out]) + list(after)
    return pl.pallas_call(
        functools.partial(last_kernel, heads),
        out_shape=[jax.ShapeDtypeStruct((tokens, width), bf16), jax.ShapeDtypeStruct((8, 128), f32)],
        in_specs=[VMEM] * (2 + 2 * n) + [ANY] * len(given),
        out_specs=[HBM, VMEM],
        scratch_shapes=[pltpu.VMEM((tokens, n * 128), bf16), pltpu.SemaphoreType.DMA((tokens // BLK,))],
        input_output_aliases={} if out is None else {2 + 2 * n: 0},
        compiler_params=PARAMS,
        cost_estimate=pl.CostEstimate(flops=n * tokens * 2 * 384 * 128, bytes_accessed=10 * tokens * 128 * n, transcendentals=tokens * n),
        name="last",
    )(gain, state, *[attn[i] for i in heads], *[scaled[i] for i in heads], *given)


def per_device(queries, keys, values, log_decay, out_gain, decode_map):
    ctx_size = lax.axis_size("ctx")
    head_size = lax.axis_size("head")

    def swap(a, mask):
        return lax.ppermute(a, "ctx", [(i, i ^ mask) for i in range(ctx_size)])

    def swap_y(a, mask):
        return lax.ppermute(a, "head", [(i, i ^ mask) for i in range(head_size)])

    tokens = queries.shape[0]
    heads = log_decay.shape[0]
    half = heads // 2
    ext = (128 + EXT, 128)
    send, keep, k_heads, v_heads = summaries(keys, values, log_decay, decode_map)
    recv = swap(send, 1)

    *t, want = small(pair_kernel, [ext] * 4 + [(8, 128)], "pair")(keep, recv)
    cr, ct = small(prep_kernel, [(heads, tokens), (tokens, heads)], "prep", (t[0],))(log_decay)
    attn, scaled = [None] * heads, [None] * heads

    def local(which, *after):
        got = local_part(which, queries, k_heads, v_heads, cr, ct, after)
        for n, i in enumerate(which):
            attn[i], scaled[i] = got[n], got[n + len(which)]
        return tuple(got[: len(which)])

    t = [t[0]] + [swap(a, 2 * d) for a, d in zip(t[1:], FAR_FIRST[1:])]
    done = local((0,), t[0])
    (g,) = small(slab_kernel, [ext], "slab", done)(*t)
    a = []
    plan = ((0, 8, (1, 2)), (1, 16, (3, 4)), (2, 48, (5, 6)))
    for bit, mask, which in plan:
        r = swap(g, mask)
        done = local(which, g)
        if bit == 0:
            want_y = swap_y(want, 1)
        if bit == 1:
            done = done + (want_y,)
        g, *a = small(functools.partial(round_kernel, bit), [ext] * 2, "round", done)(g, r, *a)
    m = small(back_kernel, [(256, 128)] * 4, "back")(g, *a, *t)
    (want_a,) = small(want_kernel, [(8, 128)], "want", (m[0],))(want, want_y)
    want_b = swap_y(want_a, 3)
    done = local((7,), m[0])
    m = [m[0]] + [swap(a, 2 * d) for a, d in zip(m[1:], FAR_FIRST[1:])]
    own, other, slots = small(
        spread_kernel, [(half, 128, 128), (half, 144, 128), (4, 16, 128)], "spread", done
    )(want_a, want_b, *m, keep, recv)
    other = swap(other, 1)

    gain = out_gain.reshape(1, -1)
    out, mark = last_part((0, 1), gain, own, attn, scaled)
    slot_send, near, far = small(merge_kernel, [(2, 16, 128), (16, 128), (16, 128)], "merge", (mark,))(slots, other)
    got = swap_y(slot_send, 1)
    out, mark = last_part((2, 3), gain, own, attn, scaled, out, (near,))
    near, far = small(slots_kernel, [(16, 128)] * 2, "slots", (mark,))(got, near, far)
    got = swap_y(far, 3)
    out, mark = last_part((4, 5, 6, 7), gain, other, attn, scaled, out, (near,))
    (decode_state,) = small(add_kernel, [(16, 128)], "sum", (mark,))(near, got)
    return (out, decode_state)


def solution(mesh):
    return jax.shard_map(
        per_device,
        mesh=mesh,
        in_specs=(
            P("ctx", "head"),
            P("ctx", "head"),
            P("ctx", "head"),
            P("head", "ctx"),
            P("head"),
            P(("ctx", "head")),
        ),
        out_specs=(P("ctx", "head"), P(("ctx", "head"), None)),
        check_vma=False,
    )
```

time: 212 us -> 55.1 us (0.26); the launches traced: 210 us -> 55 us
  waiting for transfers between devices: 83.9 us -> 8.86 us
  local copies, waits for them, and re-layouts: 49 us -> 0.02 us
  matrix products: 21.9 us -> 0 us
  Pallas kernels: 0 us -> 20.4 us
  between operations: 15.2 us -> 1.48 us
  other arithmetic: 10.3 us -> 0 us
  starting transfers between devices: 29 us -> 24.2 us
    all_gather x1 -> x0, waiting for transfers between devices: 67.5 us -> none  [per_device(): lax.all_gather(last_rows[0, 0], ('ctx', 'head'), axis=0, tiled=True)]
    all_to_all x3 -> x0, starting transfers between devices: 28.8 us -> none  [the longest x1 11.6 us: per_device(): lax.all_to_all(rows_decay, 'ctx', split_axis=0, concat_axis=1, tiled=True)]
    ppermute x0 -> x15, starting transfers between devices: none -> 24.2 us  [the longest x11 16.5 us: swap(): return lax.ppermute(a, 'ctx', [(i, i ^ mask) for i in range(ctx_size)])]
    dot_general x34 -> x0, matrix products: 21.9 us -> none  [the longest x32 11.7 us: block_local(): jnp.dot(probs, v_block[:, first_col:last_col], preferred_element_type=jnp...]
    pallas_call x0 -> x22, Pallas kernels: none -> 20.4 us  [the longest x5 10.2 us: local_part(): pl.pallas_call(body, out_shape=[jax.ShapeDtypeStruct((tokens, 128), f32)]...]
    unnamed x9 -> x6, local copies, waits for them, and re-layouts: 19.7 us -> 0.02 us
    all_to_all x3 -> x0, waiting for transfers between devices: 16.4 us -> none  [the longest x1 16.4 us: per_device(): lax.all_to_all(rows_state, 'ctx', split_axis=0, concat_axis=1, tiled=True)]
    squeeze x8 -> x0, local copies, waits for them, and re-layouts: 9.41 us -> none  [per_device(): lax.map(lambda parts: block_local(parts, heads, size), (q_blocks, k_block...]
  transfers between devices with their start and end apart: 4 -> 15, of which waited for: 2 -> 8; matrix products, arithmetic and copies ran while one was open for 30% -> 0% of each run, Pallas kernels for 0% -> 29%
where the time goes in v2:
time: 55.1 us; the launch traced here: 55 us
  starting transfers between devices  24.2 us (44%)
  Pallas kernels  20.4 us (37%)
  waiting for transfers between devices  8.86 us (16%)
  between operations  1.48 us (3%)
    ppermute x11, starting transfers between devices, swap(): return lax.ppermute(a, 'ctx', [(i, i ^ mask) for i in range(ctx_size)])  16.5 us
    pallas_call x5, Pallas kernels, local_part(): pl.pallas_call(body, out_shape=[jax.ShapeDtypeStruct((tokens, 128), f32)]...  10.2 us
    ppermute x4, starting transfers between devices, swap_y(): return lax.ppermute(a, 'head', [(i, i ^ mask) for i in range(head_size)])  7.68 us
    ppermute x11, waiting for transfers between devices, swap(): return lax.ppermute(a, 'ctx', [(i, i ^ mask) for i in range(ctx_size)])  6.37 us
    pallas_call x3, Pallas kernels, last_part(): pl.pallas_call(functools.partial(last_kernel, heads), out_shape=[jax.Shap...  4.79 us
    pallas_call x1, Pallas kernels, summaries(): pl.pallas_call(send_kernel, out_shape=[out, jax.ShapeDtypeStruct((heads,...  3.13 us
    ppermute x4, waiting for transfers between devices, swap_y(): return lax.ppermute(a, 'head', [(i, i ^ mask) for i in range(head_size)])  2.49 us
    pallas_call x12, Pallas kernels, call(): pl.pallas_call(body, out_shape=[jax.ShapeDtypeStruct(s, f32) for s in out...  1.6 us
  transfers between devices with their start and end apart: 15, of which 8 were waited for; matrix products, arithmetic and copies ran while one was open for 0% of the time, Pallas kernels for 29%

profile of v2, /device:TPU:32, one launch (start us, length us, event | category | flops | bytes accessed | tf_op | source)
XLA Modules:
  0.0 55.0 jit_solution(17320787593715200498)
XLA Ops:
  1.3 3.1 %summary_send.1 = (f32[4,136,128]{2,1,0:T(8,128)S(1)}, f32[8,1024]{1,0:T(8,128)S(1)}, f32[16,128]{1,0:T(8,128)S(1)}, bf16[8,1024,128]{2,1,0:T(8,128)(2,1)S(1)}, bf16[8,1024,128]{2,1,0:T(8,128)(2,1)S(1)}) custom-call(bf16[1024,1024]{1,0:T(8,128)(2,1)} %k_hbm.1, bf16[1024,1024]{1,0:T(8,128)(2,1)} %v_hbm.1, f32[8,1024]{1,0:T(8,128)} %refs_0_.6, s32[1]{0:T(128)S(6)} %copy.12.map_ref), custom_call_target="tpu_custom_call" | custom-call | flops 268435456 | bytes 2097152 | tf_op jit(solution)/shard_map/summary_send/pallas_call | solution.py:138
  4.5 0.8 %summary_keep.1.refs_0_.refs_6_ = f32[4,136,128]{2,1,0:T(8,128)S(1)} custom-call(bf16[8,1024,128]{2,1,0:T(8,128)(2,1)S(1)} %get-tuple-element.54.k_ref.refs_1_, bf16[8,1024,128]{2,1,0:T(8,128)(2,1)S(1)} %get-tuple-element.55.v_ref.refs_2_, f32[8,1024]{1,0:T(8,128)S(1)} %get-tuple-element.56.w_ref, f32[16,128]{1,0:T(8,128)S(1)} %get-tuple-element.57.tot_ref), custom_call_target="tpu_custom_call" | custom-call | flops 268435456 | bytes 2097152 | tf_op jit(solution)/shard_map/summary_keep/pallas_call | solution.py:158
  5.3 0.8 %collective-permute-done.refs_1_.refs_7_ = f32[4,136,128]{2,1,0:T(8,128)S(1)} collective-permute-done((f32[4,136,128]{2,1,0:T(8,128)S(1)}, f32[4,136,128]{2,1,0:T(8,128)S(1)}, u32[]{:S(2)}, u32[]{:S(2)}) %collective-permute-start) | collective-permute-done | bytes 278560 | tf_op jit(solution)/shard_map/ppermute | solution.py:431
  6.1 3.1 %collective-permute-start.2 = (f32[136,128]{1,0:T(8,128)S(1)}, f32[136,128]{1,0:T(8,128)S(1)}, u32[]{:S(2)}, u32[]{:S(2)}) collective-permute-start(f32[136,128]{1,0:T(8,128)S(1)} %get-tuple-element.61), channel_id=1, source_target_pairs={{0,16},{4,20},{8,24},{12,28},{16,0},{20,4},{24,8},{28,12},{32,48},... | collective-permute-start | bytes 208904 | tf_op jit(solution)/shard_map/ppermute | solution.py:431
  9.2 0.6 %collective-permute-start.3 = (f32[136,128]{1,0:T(8,128)S(1)}, f32[136,128]{1,0:T(8,128)S(1)}, u32[]{:S(2)}, u32[]{:S(2)}) collective-permute-start(f32[136,128]{1,0:T(8,128)S(1)} %get-tuple-element.62), channel_id=1, source_target_pairs={{0,8},{4,12},{8,0},{12,4},{16,24},{20,28},{24,16},{28,20},{32,40},... | collective-permute-start | bytes 208904 | tf_op jit(solution)/shard_map/ppermute | solution.py:431
  9.8 0.5 collective-permute-start.4
  10.4 0.4 prep.1
  10.7 1.5 %local_attn.5 = (f32[1024,128]{1,0:T(8,128)S(1)}, bf16[1024,256]{1,0:T(8,128)(2,1)S(1)}) custom-call(bf16[1024,1024]{1,0:T(8,128)(2,1)S(1)} %copy-done, bf16[8,1024,128]{2,1,0:T(8,128)(2,1)S(1)} %get-tuple-element.54.k_ref.refs_1_, bf16[8,1024,128]{2,1,0:T(8,128)(2,1)S(1)} %get-tuple-element.55.v_ref.refs_2_, f32[8,1024]{1,0:T(8,128)S(1)} %get-tuple-element.64.refs_3_, ...), custom_call_target="tpu_custom_call" | custom-call | flops 201326592 | bytes 1310720 | tf_op jit(solution)/shard_map/local_attn/pallas_call | solution.py:369
  12.2 1.4 %collective-permute-done.3.refs_2_.refs_4_ = f32[136,128]{1,0:T(8,128)S(1)} collective-permute-done((f32[136,128]{1,0:T(8,128)S(1)}, f32[136,128]{1,0:T(8,128)S(1)}, u32[]{:S(2)}, u32[]{:S(2)}) %collective-permute-start.3) | collective-permute-done | bytes 69664 | tf_op jit(solution)/shard_map/ppermute | solution.py:431
  13.6 1.7 %collective-permute-done.4.refs_3_.refs_5_ = f32[136,128]{1,0:T(8,128)S(1)} collective-permute-done((f32[136,128]{1,0:T(8,128)S(1)}, f32[136,128]{1,0:T(8,128)S(1)}, u32[]{:S(2)}, u32[]{:S(2)}) %collective-permute-start.4) | collective-permute-done | bytes 69664 | tf_op jit(solution)/shard_map/ppermute | solution.py:431
  15.6 2.4 %local_attn.6 = (f32[1024,128]{1,0:T(8,128)S(1)}, f32[1024,128]{1,0:T(8,128)S(1)}, bf16[1024,256]{1,0:T(8,128)(2,1)S(1)}, bf16[1024,256]{1,0:T(8,128)(2,1)S(1)}) custom-call(bf16[1024,1024]{1,0:T(8,128)(2,1)S(1)} %copy-done, bf16[8,1024,128]{2,1,0:T(8,128)(2,1)S(1)} %get-tuple-element.54.k_ref.refs_1_, ...), custom_call_target="tpu_custom_call" | custom-call | flops 402653184 | bytes 2621440 | tf_op jit(solution)/shard_map/local_attn/pallas_call | solution.py:369
  18.0 1.8 %collective-permute-done.5.refs_1_ = f32[136,128]{1,0:T(8,128)S(1)} collective-permute-done((f32[136,128]{1,0:T(8,128)S(1)}, f32[136,128]{1,0:T(8,128)S(1)}, u32[]{:S(2)}, u32[]{:S(2)}) %collective-permute-start.5) | collective-permute-done | bytes 69664 | tf_op jit(solution)/shard_map/ppermute | solution.py:431
  19.8 3.4 %collective-permute-start.6 = (f32[136,128]{1,0:T(8,128)S(1)}, f32[136,128]{1,0:T(8,128)S(1)}, u32[]{:S(2)}, u32[]{:S(2)}) collective-permute-start(f32[136,128]{1,0:T(8,128)S(1)} %get-tuple-element.69.refs_5_.refs_0_), channel_id=1, source_target_pairs={{0,64},{4,68},{8,72},{12,76},{16,80},{20,84},{24,88},{28,92},{32,9... | collective-permute-start | bytes 208904 | tf_op jit(solution)/shard_map/ppermute | solution.py:431
  23.2 1.6 %collective-permute-start.1 = (f32[8,128]{1,0:T(8,128)S(1)}, f32[8,128]{1,0:T(8,128)S(1)}, u32[]{:S(2)}, u32[]{:S(2)}) collective-permute-start(f32[8,128]{1,0:T(8,128)S(1)} %get-tuple-element.59.refs_0_), channel_id=1, source_target_pairs={{0,1},{1,0},{2,3},{3,2},{4,5},{5,4},{6,7},{7,6},{8,9},{9,8},{10,11... | collective-permute-start | bytes 12296 | tf_op jit(solution)/shard_map/ppermute | solution.py:434
  24.7 2.4 %local_attn.7 = (f32[1024,128]{1,0:T(8,128)S(1)}, f32[1024,128]{1,0:T(8,128)S(1)}, bf16[1024,256]{1,0:T(8,128)(2,1)S(1)}, bf16[1024,256]{1,0:T(8,128)(2,1)S(1)}) custom-call(bf16[1024,1024]{1,0:T(8,128)(2,1)S(1)} %copy-done, bf16[8,1024,128]{2,1,0:T(8,128)(2,1)S(1)} %get-tuple-element.54.k_ref.refs_1_, ...), custom_call_target="tpu_custom_call" | custom-call | flops 402653184 | bytes 2621440 | tf_op jit(solution)/shard_map/local_attn/pallas_call | solution.py:369
  27.2 4.3 %collective-permute-start.7 = (f32[136,128]{1,0:T(8,128)S(1)}, f32[136,128]{1,0:T(8,128)S(1)}, u32[]{:S(2)}, u32[]{:S(2)}) collective-permute-start(f32[136,128]{1,0:T(8,128)S(1)} %get-tuple-element.73.refs_5_.refs_0_), channel_id=1, source_target_pairs={{0,192},{4,196},{8,200},{12,204},{16,208},{20,212},{24,216},{28,22... | collective-permute-start | bytes 208904 | tf_op jit(solution)/shard_map/ppermute | solution.py:431
  31.6 2.4 %local_attn.8 = (f32[1024,128]{1,0:T(8,128)S(1)}, f32[1024,128]{1,0:T(8,128)S(1)}, bf16[1024,256]{1,0:T(8,128)(2,1)S(1)}, bf16[1024,256]{1,0:T(8,128)(2,1)S(1)}) custom-call(bf16[1024,1024]{1,0:T(8,128)(2,1)S(1)} %copy-done, bf16[8,1024,128]{2,1,0:T(8,128)(2,1)S(1)} %get-tuple-element.54.k_ref.refs_1_, ...), custom_call_target="tpu_custom_call" | custom-call | flops 402653184 | bytes 2621440 | tf_op jit(solution)/shard_map/local_attn/pallas_call | solution.py:369
  34.0 0.6 %collective-permute-done.7.refs_1_ = f32[136,128]{1,0:T(8,128)S(1)} collective-permute-done((f32[136,128]{1,0:T(8,128)S(1)}, f32[136,128]{1,0:T(8,128)S(1)}, u32[]{:S(2)}, u32[]{:S(2)}) %collective-permute-start.7) | collective-permute-done | bytes 69664 | tf_op jit(solution)/shard_map/ppermute | solution.py:431
  34.7 1.2 %collective-permute-start.9 = (f32[256,128]{1,0:T(8,128)S(1)}, f32[256,128]{1,0:T(8,128)S(1)}, u32[]{:S(2)}, u32[]{:S(2)}) collective-permute-start(f32[256,128]{1,0:T(8,128)S(1)} %get-tuple-element.80), channel_id=1, source_target_pairs={{0,16},{4,20},{8,24},{12,28},{16,0},{20,4},{24,8},{28,12},{32,48},... | collective-permute-start | bytes 393224 | tf_op jit(solution)/shard_map/ppermute | solution.py:431
  35.9 0.7 %collective-permute-start.10 = (f32[256,128]{1,0:T(8,128)S(1)}, f32[256,128]{1,0:T(8,128)S(1)}, u32[]{:S(2)}, u32[]{:S(2)}) collective-permute-start(f32[256,128]{1,0:T(8,128)S(1)} %get-tuple-element.81), channel_id=1, source_target_pairs={{0,8},{4,12},{8,0},{12,4},{16,24},{20,28},{24,16},{28,20},{32,40},... | collective-permute-start | bytes 393224 | tf_op jit(solution)/shard_map/ppermute | solution.py:431
  36.6 2.3 %collective-permute-start.11 = (f32[256,128]{1,0:T(8,128)S(1)}, f32[256,128]{1,0:T(8,128)S(1)}, u32[]{:S(2)}, u32[]{:S(2)}) collective-permute-start(f32[256,128]{1,0:T(8,128)S(1)} %get-tuple-element.82), channel_id=1, source_target_pairs={{0,24},{4,28},{8,16},{12,20},{16,8},{20,12},{24,0},{28,4},{32,56},... | collective-permute-start | bytes 393224 | tf_op jit(solution)/shard_map/ppermute | solution.py:431
  38.9 2.8 %collective-permute-start.8 = (f32[8,128]{1,0:T(8,128)S(1)}, f32[8,128]{1,0:T(8,128)S(1)}, u32[]{:S(2)}, u32[]{:S(2)}) collective-permute-start(f32[8,128]{1,0:T(8,128)S(1)} %want.1.refs_0_), channel_id=1, source_target_pairs={{0,3},{1,2},{2,1},{3,0},{4,7},{5,6},{6,5},{7,4},{8,11},{9,10},{10,... | collective-permute-start | bytes 12296 | tf_op jit(solution)/shard_map/ppermute | solution.py:434
  41.7 1.4 %local_attn.9 = (f32[1024,128]{1,0:T(8,128)S(1)}, bf16[1024,256]{1,0:T(8,128)(2,1)S(1)}) custom-call(bf16[1024,1024]{1,0:T(8,128)(2,1)S(1)} %copy-done, bf16[8,1024,128]{2,1,0:T(8,128)(2,1)S(1)} %get-tuple-element.54.k_ref.refs_1_, bf16[8,1024,128]{2,1,0:T(8,128)(2,1)S(1)} %get-tuple-element.55.v_ref.refs_2_, f32[8,1024]{1,0:T(8,128)S(1)} %get-tuple-element.64.refs_3_, ...), custom_call_target="tpu_custom_call" | custom-call | flops 201326592 | bytes 1310720 | tf_op jit(solution)/shard_map/local_attn/pallas_call | solution.py:369
  43.2 0.5 collective-permute-done.8.refs_1_
  43.7 0.4 spread.1
  44.2 1.4 %last.3 = (bf16[1024,1024]{1,0:T(8,128)(2,1)}, f32[8,128]{1,0:T(8,128)S(1)}) custom-call(f32[1,1024]{1,0:T(1,128)S(1)} %bitcast.1, f32[4,128,128]{2,1,0:T(8,128)S(1)} %get-tuple-element.89.p_ref, f32[1024,128]{1,0:T(8,128)S(1)} %get-tuple-element.66.refs_4_.rest_0_, f32[1024,128]{1,0:T(8,128)S(1)} %get-tuple-element.67.refs_2_.rest_1_, ...), custom_call_target="tpu_custom_call" | custom-call | flops 201326592 | bytes 2621440 | tf_op jit(solution)/shard_map/last/pallas_call | solution.py:413
  45.8 0.4 collective-permute-start.13
  46.2 1.4 %last.4 = (bf16[1024,1024]{1,0:T(8,128)(2,1)}, f32[8,128]{1,0:T(8,128)S(1)}) custom-call(f32[1,1024]{1,0:T(1,128)S(1)} %bitcast.2, f32[4,128,128]{2,1,0:T(8,128)S(1)} %get-tuple-element.89.p_ref, f32[1024,128]{1,0:T(8,128)S(1)} %get-tuple-element.68.refs_3_.rest_0_, ...), custom_call_target="tpu_custom_call", output_to_operand_aliasing={{0}: (6, {})} | custom-call | flops 201326592 | bytes 2621440 | tf_op jit(solution)/shard_map/last/pallas_call | solution.py:413
  47.6 1.9 %collective-permute-done.13.refs_0_ = f32[2,16,128]{2,1,0:T(8,128)S(1)} collective-permute-done((f32[2,16,128]{2,1,0:T(8,128)S(1)}, f32[2,16,128]{2,1,0:T(8,128)S(1)}, u32[]{:S(2)}, u32[]{:S(2)}) %collective-permute-start.13) | collective-permute-done | bytes 16416 | tf_op jit(solution)/shard_map/ppermute | solution.py:434
  49.5 2.8 %collective-permute-start.14 = (f32[16,128]{1,0:T(8,128)S(1)}, f32[16,128]{1,0:T(8,128)S(1)}, u32[]{:S(2)}, u32[]{:S(2)}) collective-permute-start(f32[16,128]{1,0:T(8,128)S(1)} %get-tuple-element.104), channel_id=1, source_target_pairs={{0,3},{1,2},{2,1},{3,0},{4,7},{5,6},{6,5},{7,4},{8,11},{9,10},{10,... | collective-permute-start | bytes 24584 | tf_op jit(solution)/shard_map/ppermute | solution.py:434
  52.3 2.0 %last.5 = (bf16[1024,1024]{1,0:T(8,128)(2,1)}, f32[8,128]{1,0:T(8,128)S(1)}) custom-call(f32[1,1024]{1,0:T(1,128)S(1)} %bitcast.3, f32[4,144,128]{2,1,0:T(8,128)S(1)} %collective-permute-done.12.refs_1_.p_ref, f32[1024,128]{1,0:T(8,128)S(1)} %get-tuple-element.72.refs_4_.rest_0_, ...), custom_call_target="tpu_custom_call", output_to_operand_aliasing={{0}: (10, {})} | custom-call | flops 402653184 | bytes 5242880 | tf_op jit(solution)/shard_map/last/pallas_call | solution.py:413
  54.4 0.6 %sum.1 = f32[16,128]{1,0:T(8,128)} custom-call(f32[16,128]{1,0:T(8,128)S(1)} %get-tuple-element.102.rest_9_.refs_0_, f32[16,128]{1,0:T(8,128)S(1)} %collective-permute-done.14.refs_1_, f32[8,128]{1,0:T(8,128)S(1)} %get-tuple-element.105.refs_2_), custom_call_target="tpu_custom_call" | custom-call | tf_op jit(solution)/shard_map/sum/pallas_call | solution.py:299
  (26 shorter events, 0.9 us)
Async XLA Ops:
  4.4 1.6 %collective-permute-start = (f32[4,136,128]{2,1,0:T(8,128)S(1)}, f32[4,136,128]{2,1,0:T(8,128)S(1)}, u32[]{:S(2)}, u32[]{:S(2)}) collective-permute-start(f32[4,136,128]{2,1,0:T(8,128)S(1)} %get-tuple-element.58), channel_id=1, source_target_pairs={{0,4},{4,0},{8,12},{12,8},{16,20},{20,16},{24,28},{28,24},{32,36},... | collective-permute-start | bytes 835592 | tf_op jit(solution)/shard_map/ppermute | solution.py:431
  4.5 5.9 %copy-start.1 = (f32[8,1024]{1,0:T(8,128)S(1)}, f32[8,1024]{1,0:T(8,128)}, u32[]{:S(2)}) copy-start(f32[8,1024]{1,0:T(8,128)} %refs_0_.6) | copy-start | bytes 98308
  4.5 6.2 %copy-start = (bf16[1024,1024]{1,0:T(8,128)(2,1)S(1)}, bf16[1024,1024]{1,0:T(8,128)(2,1)}, u32[]{:S(2)}) copy-start(bf16[1024,1024]{1,0:T(8,128)(2,1)} %refs_0_.11) | copy-start | bytes 6291460
  6.1 6.1 %collective-permute-start.2 = (f32[136,128]{1,0:T(8,128)S(1)}, f32[136,128]{1,0:T(8,128)S(1)}, u32[]{:S(2)}, u32[]{:S(2)}) collective-permute-start(f32[136,128]{1,0:T(8,128)S(1)} %get-tuple-element.61), channel_id=1, source_target_pairs={{0,16},{4,20},{8,24},{12,28},{16,0},{20,4},{24,8},{28,12},{32,48},... | collective-permute-start | bytes 208904 | tf_op jit(solution)/shard_map/ppermute | solution.py:431
  9.2 4.4 %collective-permute-start.3 = (f32[136,128]{1,0:T(8,128)S(1)}, f32[136,128]{1,0:T(8,128)S(1)}, u32[]{:S(2)}, u32[]{:S(2)}) collective-permute-start(f32[136,128]{1,0:T(8,128)S(1)} %get-tuple-element.62), channel_id=1, source_target_pairs={{0,8},{4,12},{8,0},{12,4},{16,24},{20,28},{24,16},{28,20},{32,40},... | collective-permute-start | bytes 208904 | tf_op jit(solution)/shard_map/ppermute | solution.py:431
  9.8 5.5 %collective-permute-start.4 = (f32[136,128]{1,0:T(8,128)S(1)}, f32[136,128]{1,0:T(8,128)S(1)}, u32[]{:S(2)}, u32[]{:S(2)}) collective-permute-start(f32[136,128]{1,0:T(8,128)S(1)} %get-tuple-element.63), channel_id=1, source_target_pairs={{0,24},{4,28},{8,16},{12,20},{16,8},{20,12},{24,0},{28,4},{32,56},... | collective-permute-start | bytes 208904 | tf_op jit(solution)/shard_map/ppermute | solution.py:431
  15.4 4.4 %collective-permute-start.5 = (f32[136,128]{1,0:T(8,128)S(1)}, f32[136,128]{1,0:T(8,128)S(1)}, u32[]{:S(2)}, u32[]{:S(2)}) collective-permute-start(f32[136,128]{1,0:T(8,128)S(1)} %slab.1.refs_5_.refs_0_), channel_id=1, source_target_pairs={{0,32},{4,36},{8,40},{12,44},{16,48},{20,52},{24,56},{28,60},{32,0... | collective-permute-start | bytes 208904 | tf_op jit(solution)/shard_map/ppermute | solution.py:431
  19.8 7.4 %collective-permute-start.6 = (f32[136,128]{1,0:T(8,128)S(1)}, f32[136,128]{1,0:T(8,128)S(1)}, u32[]{:S(2)}, u32[]{:S(2)}) collective-permute-start(f32[136,128]{1,0:T(8,128)S(1)} %get-tuple-element.69.refs_5_.refs_0_), channel_id=1, source_target_pairs={{0,64},{4,68},{8,72},{12,76},{16,80},{20,84},{24,88},{28,92},{32,9... | collective-permute-start | bytes 208904 | tf_op jit(solution)/shard_map/ppermute | solution.py:431
  23.2 4.0 %collective-permute-start.1 = (f32[8,128]{1,0:T(8,128)S(1)}, f32[8,128]{1,0:T(8,128)S(1)}, u32[]{:S(2)}, u32[]{:S(2)}) collective-permute-start(f32[8,128]{1,0:T(8,128)S(1)} %get-tuple-element.59.refs_0_), channel_id=1, source_target_pairs={{0,1},{1,0},{2,3},{3,2},{4,5},{5,4},{6,7},{7,6},{8,9},{9,8},{10,11... | collective-permute-start | bytes 12296 | tf_op jit(solution)/shard_map/ppermute | solution.py:434
  27.2 7.3 %collective-permute-start.7 = (f32[136,128]{1,0:T(8,128)S(1)}, f32[136,128]{1,0:T(8,128)S(1)}, u32[]{:S(2)}, u32[]{:S(2)}) collective-permute-start(f32[136,128]{1,0:T(8,128)S(1)} %get-tuple-element.73.refs_5_.refs_0_), channel_id=1, source_target_pairs={{0,192},{4,196},{8,200},{12,204},{16,208},{20,212},{24,216},{28,22... | collective-permute-start | bytes 208904 | tf_op jit(solution)/shard_map/ppermute | solution.py:431
  34.7 9.0 %collective-permute-start.9 = (f32[256,128]{1,0:T(8,128)S(1)}, f32[256,128]{1,0:T(8,128)S(1)}, u32[]{:S(2)}, u32[]{:S(2)}) collective-permute-start(f32[256,128]{1,0:T(8,128)S(1)} %get-tuple-element.80), channel_id=1, source_target_pairs={{0,16},{4,20},{8,24},{12,28},{16,0},{20,4},{24,8},{28,12},{32,48},... | collective-permute-start | bytes 393224 | tf_op jit(solution)/shard_map/ppermute | solution.py:431
  35.9 7.8 %collective-permute-start.10 = (f32[256,128]{1,0:T(8,128)S(1)}, f32[256,128]{1,0:T(8,128)S(1)}, u32[]{:S(2)}, u32[]{:S(2)}) collective-permute-start(f32[256,128]{1,0:T(8,128)S(1)} %get-tuple-element.81), channel_id=1, source_target_pairs={{0,8},{4,12},{8,0},{12,4},{16,24},{20,28},{24,16},{28,20},{32,40},... | collective-permute-start | bytes 393224 | tf_op jit(solution)/shard_map/ppermute | solution.py:431
  36.6 7.1 %collective-permute-start.11 = (f32[256,128]{1,0:T(8,128)S(1)}, f32[256,128]{1,0:T(8,128)S(1)}, u32[]{:S(2)}, u32[]{:S(2)}) collective-permute-start(f32[256,128]{1,0:T(8,128)S(1)} %get-tuple-element.82), channel_id=1, source_target_pairs={{0,24},{4,28},{8,16},{12,20},{16,8},{20,12},{24,0},{28,4},{32,56},... | collective-permute-start | bytes 393224 | tf_op jit(solution)/shard_map/ppermute | solution.py:431
  38.9 5.3 %copy-start.2 = (f32[1024]{0:T(1024)S(1)}, f32[1024]{0:T(1024)}, u32[]{:S(2)}) copy-start(f32[1024]{0:T(1024)} %param.10) | copy-start | bytes 12292
  38.9 4.8 %collective-permute-start.8 = (f32[8,128]{1,0:T(8,128)S(1)}, f32[8,128]{1,0:T(8,128)S(1)}, u32[]{:S(2)}, u32[]{:S(2)}) collective-permute-start(f32[8,128]{1,0:T(8,128)S(1)} %want.1.refs_0_), channel_id=1, source_target_pairs={{0,3},{1,2},{2,1},{3,0},{4,7},{5,6},{6,5},{7,4},{8,11},{9,10},{10,... | collective-permute-start | bytes 12296 | tf_op jit(solution)/shard_map/ppermute | solution.py:434
  44.1 1.7 %collective-permute-start.12 = (f32[4,144,128]{2,1,0:T(8,128)S(1)}, f32[4,144,128]{2,1,0:T(8,128)S(1)}, u32[]{:S(2)}, u32[]{:S(2)}) collective-permute-start(f32[4,144,128]{2,1,0:T(8,128)S(1)} %get-tuple-element.84), channel_id=1, source_target_pairs={{0,4},{4,0},{8,12},{12,8},{16,20},{20,16},{24,28},{28,24},{32,36},... | collective-permute-start | bytes 884744 | tf_op jit(solution)/shard_map/ppermute | solution.py:431
  45.8 3.7 %collective-permute-start.13 = (f32[2,16,128]{2,1,0:T(8,128)S(1)}, f32[2,16,128]{2,1,0:T(8,128)S(1)}, u32[]{:S(2)}, u32[]{:S(2)}) collective-permute-start(f32[2,16,128]{2,1,0:T(8,128)S(1)} %get-tuple-element.99), channel_id=1, source_target_pairs={{0,1},{1,0},{2,3},{3,2},{4,5},{5,4},{6,7},{7,6},{8,9},{9,8},{10,11... | collective-permute-start | bytes 49160 | tf_op jit(solution)/shard_map/ppermute | solution.py:434
  49.5 4.9 %collective-permute-start.14 = (f32[16,128]{1,0:T(8,128)S(1)}, f32[16,128]{1,0:T(8,128)S(1)}, u32[]{:S(2)}, u32[]{:S(2)}) collective-permute-start(f32[16,128]{1,0:T(8,128)S(1)} %get-tuple-element.104), channel_id=1, source_target_pairs={{0,3},{1,2},{2,1},{3,0},{4,7},{5,6},{6,5},{7,4},{8,11},{9,10},{10,... | collective-permute-start | bytes 24584 | tf_op jit(solution)/shard_map/ppermute | solution.py:434

commit v3 on v2

--- a/solution.py
+++ b/solution.py
@@ -66,6 +66,10 @@
     return jnp.where(core == 0, ld, jnp.concatenate([ld[half:], ld[:half]], axis=0))
 
 
+def head_column(i, heads):
+    return pl.multiple_of(((i + heads // 2 * place()[0]) % heads) * 128, 128)
+
+
 def state_sum(k, v, w):
     kt = k.T.astype(f32) * w
     hi, lo = split2(kt)
@@ -86,22 +90,20 @@
     half = heads // 2
     ld_copy = pltpu.make_async_copy(ld_hbm, ld_buf, ld_sem)
     ld_copy.start()
-    copies = {}
-
-    def fetch(i):
-        col = pl.multiple_of(((i + half * core) % heads) * 128, 128)
-        copies[i] = [
-            pltpu.make_async_copy(src.at[:, pl.ds(col, 128)], buf.at[i], sems.at[n, i])
-            for n, (src, buf) in enumerate(((k_hbm, k_ref), (v_hbm, v_ref)))
-        ]
-        for copy in copies[i]:
+    def fetch(side):
+        cols = pl.ds(pl.multiple_of(((side + core) % 2) * half * 128, half * 128), half * 128)
+        copies = []
+        for r in range(sems.shape[2]):
+            rows = pl.ds(r * (tokens // sems.shape[2]), tokens // sems.shape[2])
+            for n, (src, buf) in enumerate(((k_hbm, k_ref), (v_hbm, v_ref))):
+                copies.append(pltpu.make_async_copy(src.at[rows, cols], buf.at[rows, cols], sems.at[n, side, r]))
+        for copy in copies:
             copy.start()
-
-    for i in range(half, heads):
-        fetch(i)
+        return copies
+
+    sent = fetch(1)
     ld_copy.wait()
-    for i in range(half):
-        fetch(i)
+    kept = fetch(0)
     ld = kept_first(ld_buf[...], core)
     n = tokens // BLK
     cums = block_cums(ld)
@@ -112,19 +114,20 @@
         after = after + total
     tot_ref[0:heads, :] = jnp.broadcast_to(after, (heads, 128))
     tot_ref[heads:, :] = jnp.full((8, 128), map_ref[0], jnp.int32).astype(f32)
+    for copy in sent:
+        copy.wait()
     for i in range(half):
         h = i + half
-        for copy in copies[h]:
-            copy.wait()
-        write_sum(s_ref, i, state_sum(k_ref[h], v_ref[h], w_ref[h : h + 1, :]), tot_ref, h)
-    for i in range(half):
-        for copy in copies[i]:
-            copy.wait()
+        cols = pl.ds(head_column(h, heads), 128)
+        write_sum(s_ref, i, state_sum(k_ref[:, cols], v_ref[:, cols], w_ref[h : h + 1, :]), tot_ref, h)
+    for copy in kept:
+        copy.wait()
 
 
 def keep_kernel(k_ref, v_ref, w_ref, tot_ref, s_ref):
     for i in range(s_ref.shape[0]):
-        write_sum(s_ref, i, state_sum(k_ref[i], v_ref[i], w_ref[i : i + 1, :]), tot_ref, i)
+        cols = pl.ds(head_column(i, 2 * s_ref.shape[0]), 128)
+        write_sum(s_ref, i, state_sum(k_ref[:, cols], v_ref[:, cols], w_ref[i : i + 1, :]), tot_ref, i)
 
 
 def summaries(keys, values, ld, decode_map):
@@ -132,7 +135,6 @@
     heads = ld.shape[0]
     half = heads // 2
     out = jax.ShapeDtypeStruct((half, 128 + EXT, 128), f32)
-    by_head = jax.ShapeDtypeStruct((heads, tokens, 128), bf16)
     cost = pl.CostEstimate(flops=2 * 2 * half * tokens * 128 * 128, bytes_accessed=2 * tokens * heads * 128, transcendentals=0)
     inputs = [pltpu.with_memory_space_constraint(a, pltpu.HBM) for a in (keys, values, ld)]
     send, w, tot, k_heads, v_heads = pl.pallas_call(
@@ -141,14 +143,14 @@
             out,
             jax.ShapeDtypeStruct((heads, tokens), f32),
             jax.ShapeDtypeStruct((heads + 8, 128), f32),
-            by_head,
-            by_head,
+            jax.ShapeDtypeStruct(keys.shape, bf16),
+            jax.ShapeDtypeStruct(keys.shape, bf16),
         ],
         in_specs=[HBM, HBM, HBM, SMEM],
         out_specs=[VMEM] * 5,
         scratch_shapes=[
             pltpu.VMEM((heads, tokens), f32),
-            pltpu.SemaphoreType.DMA((2, heads)),
+            pltpu.SemaphoreType.DMA((2, 2, 1)),
             pltpu.SemaphoreType.DMA(()),
         ],
         compiler_params=PARAMS,
@@ -319,7 +321,6 @@
 
 
 def local_kernel(heads, q_ref, k_ref, v_ref, cr_ref, ct_ref, *rest):
-    core = place()[0]
     total_heads, tokens = cr_ref.shape
     outs, scaled = rest[: len(heads)], rest[len(heads) :]
     h2 = BLK // 2
@@ -327,12 +328,12 @@
     col = lax.broadcasted_iota(jnp.int32, (h2, h2), 1)
     causal = row >= col
     for i, out, qs in zip(heads, outs, scaled):
-        at = pl.multiple_of(((i + total_heads // 2 * core) % total_heads) * 128, 128)
+        at = head_column(i, total_heads)
         run = None
         off = jnp.zeros((1, 1), f32)
         for j in range(tokens // BLK):
             rows = slice(j * BLK, (j + 1) * BLK)
-            q, k, v = q_ref[rows, pl.ds(at, 128)], k_ref[i, rows, :], v_ref[i, rows, :]
+            q, k, v = q_ref[rows, pl.ds(at, 128)], k_ref[rows, pl.ds(at, 128)], v_ref[rows, pl.ds(at, 128)]
             c_row = cr_ref[i : i + 1, rows]
             c_col = ct_ref[rows, i : i + 1]
             total = c_row[:, BLK - 1 : BLK]
@@ -341,20 +342,24 @@
             qs[rows, 0:128] = hi
             qs[rows, 128:256] = lo
             off = off + total
-            for t in range(2):
-                part = slice(t * h2, (t + 1) * h2)
-                seen = (t + 1) * h2
-                scores = lax.dot_general(q[part], k[:seen], (((1,), (1,)), ((), ())), preferred_element_type=f32)
-                gap = c_col[part] - c_row[:, :seen]
-                inner = jnp.where(causal, jnp.exp2(jnp.where(causal, gap[:, t * h2 :], 0.0)), 0.0)
-                weights = inner if t == 0 else jnp.concatenate([jnp.exp2(gap[:, :h2]), inner], axis=1)
-                attn = dot((scores * weights).astype(bf16), v[:seen])
-                if run is not None:
-                    twice = jnp.concatenate([q[part], q[part]], axis=1)
-                    attn = attn + dot(twice, halves) * decay[part]
-                out[j * BLK + t * h2 : j * BLK + seen, :] = attn
-            if j + 1 < tokens // BLK:
-                new = state_sum(k, v, jnp.exp2(total - c_row))
+            scores = lax.dot_general(q, k, (((1,), (1,)), ((), ())), preferred_element_type=f32)
+            gap = c_col - c_row
+            top = jnp.where(causal, jnp.exp2(gap[:h2, :h2]) * scores[:h2, :h2], 0.0)
+            low = jnp.exp2(gap[h2:, :h2]) * scores[h2:, :h2]
+            end = jnp.where(causal, jnp.exp2(gap[h2:, h2:]) * scores[h2:, h2:], 0.0)
+            left = jnp.concatenate([top.astype(bf16), low.astype(bf16)], axis=0)
+            right = jnp.concatenate([jnp.zeros((h2, h2), bf16), end.astype(bf16)], axis=0)
+            mixed = [jnp.concatenate([left, right], axis=1)]
+            more = j + 1 < tokens // BLK
+            if more:
+                mixed += split2(k.T.astype(f32) * jnp.exp2(total - c_row))
+            mixed = dot(jnp.concatenate(mixed, axis=0), v)
+            attn = mixed[:BLK]
+            if run is not None:
+                attn = attn + dot(jnp.concatenate([q, q], axis=1), halves) * decay
+            out[rows, :] = attn
+            if more:
+                new = mixed[BLK : BLK + 128] + mixed[BLK + 128 :]
                 run = new if run is None else run * jnp.exp2(total) + new
                 halves = jnp.concatenate(split2(run), axis=0)
 

time: 55.1 us -> 54.5 us (0.989)
  Pallas kernels: 20.4 us -> 18.4 us
  starting transfers between devices: 24.2 us -> 25 us
  waiting for transfers between devices: 8.86 us -> 9.42 us
    pallas_call x5, Pallas kernels: 10.2 us -> 8.45 us  [local_part(): pl.pallas_call(body, out_shape=[jax.ShapeDtypeStruct((tokens, 128), f32)]...]
    ppermute x11, waiting for transfers between devices: 6.37 us -> 7 us  [swap(): return lax.ppermute(a, 'ctx', [(i, i ^ mask) for i in range(ctx_size)])]
  transfers between devices with their start and end apart: 15 -> 15, of which waited for: 8 -> 9; matrix products, arithmetic and copies ran while one was open for 0% -> 0% of each run, Pallas kernels for 29% -> 27%
where the time goes in v3:
time: 54.5 us; the launch traced here: 54.4 us
  starting transfers between devices  25 us (46%)
  Pallas kernels  18.4 us (34%)
  waiting for transfers between devices  9.42 us (17%)
  between operations  1.48 us (3%)
    ppermute x11, starting transfers between devices, swap(): return lax.ppermute(a, 'ctx', [(i, i ^ mask) for i in range(ctx_size)])  16.8 us
    pallas_call x5, Pallas kernels, local_part(): pl.pallas_call(body, out_shape=[jax.ShapeDtypeStruct((tokens, 128), f32)]...  8.45 us
    ppermute x4, starting transfers between devices, swap_y(): return lax.ppermute(a, 'head', [(i, i ^ mask) for i in range(head_size)])  8.19 us
    ppermute x11, waiting for transfers between devices, swap(): return lax.ppermute(a, 'ctx', [(i, i ^ mask) for i in range(ctx_size)])  7 us
    pallas_call x3, Pallas kernels, last_part(): pl.pallas_call(functools.partial(last_kernel, heads), out_shape=[jax.Shap...  4.79 us
    pallas_call x1, Pallas kernels, summaries(): pl.pallas_call(send_kernel, out_shape=[out, jax.ShapeDtypeStruct((heads,...  2.59 us
    ppermute x4, waiting for transfers between devices, swap_y(): return lax.ppermute(a, 'head', [(i, i ^ mask) for i in range(head_size)])  2.42 us
    pallas_call x12, Pallas kernels, call(): pl.pallas_call(body, out_shape=[jax.ShapeDtypeStruct(s, f32) for s in out...  1.6 us
  transfers between devices with their start and end apart: 15, of which 9 were waited for; matrix products, arithmetic and copies ran while one was open for 0% of the time, Pallas kernels for 27%

profile of v3, /device:TPU:32, one launch (start us, length us, event | category | flops | bytes accessed | tf_op | source)
XLA Modules:
  0.0 54.4 jit_solution(16152437718804367804)
XLA Ops:
  1.3 2.6 %summary_send.1 = (f32[4,136,128]{2,1,0:T(8,128)S(1)}, f32[8,1024]{1,0:T(8,128)S(1)}, f32[16,128]{1,0:T(8,128)S(1)}, bf16[1024,1024]{1,0:T(8,128)(2,1)S(1)}, bf16[1024,1024]{1,0:T(8,128)(2,1)S(1)}) custom-call(bf16[1024,1024]{1,0:T(8,128)(2,1)} %k_hbm.1, bf16[1024,1024]{1,0:T(8,128)(2,1)} %v_hbm.1, f32[8,1024]{1,0:T(8,128)} %refs_0_.6, s32[1]{0:T(128)S(6)} %copy.12.map_ref), custom_call_target="tpu_custom_call" | custom-call | flops 268435456 | bytes 2097152 | tf_op jit(solution)/shard_map/summary_send/pallas_call | solution.py:140
  4.0 1.0 %summary_keep.1.refs_0_.refs_6_ = f32[4,136,128]{2,1,0:T(8,128)S(1)} custom-call(bf16[1024,1024]{1,0:T(8,128)(2,1)S(1)} %get-tuple-element.54.k_ref.refs_1_, bf16[1024,1024]{1,0:T(8,128)(2,1)S(1)} %get-tuple-element.55.v_ref.refs_2_, f32[8,1024]{1,0:T(8,128)S(1)} %get-tuple-element.56.w_ref, f32[16,128]{1,0:T(8,128)S(1)} %get-tuple-element.57.tot_ref), custom_call_target="tpu_custom_call" | custom-call | flops 268435456 | bytes 2097152 | tf_op jit(solution)/shard_map/summary_keep/pallas_call | solution.py:160
  5.0 0.5 collective-permute-done.refs_1_.refs_7_
  5.6 3.1 %collective-permute-start.2 = (f32[136,128]{1,0:T(8,128)S(1)}, f32[136,128]{1,0:T(8,128)S(1)}, u32[]{:S(2)}, u32[]{:S(2)}) collective-permute-start(f32[136,128]{1,0:T(8,128)S(1)} %get-tuple-element.61), channel_id=1, source_target_pairs={{0,16},{4,20},{8,24},{12,28},{16,0},{20,4},{24,8},{28,12},{32,48},... | collective-permute-start | bytes 208904 | tf_op jit(solution)/shard_map/ppermute | solution.py:436
  8.7 0.6 %collective-permute-start.3 = (f32[136,128]{1,0:T(8,128)S(1)}, f32[136,128]{1,0:T(8,128)S(1)}, u32[]{:S(2)}, u32[]{:S(2)}) collective-permute-start(f32[136,128]{1,0:T(8,128)S(1)} %get-tuple-element.62), channel_id=1, source_target_pairs={{0,8},{4,12},{8,0},{12,4},{16,24},{20,28},{24,16},{28,20},{32,40},... | collective-permute-start | bytes 208904 | tf_op jit(solution)/shard_map/ppermute | solution.py:436
  9.3 0.6 %collective-permute-start.4 = (f32[136,128]{1,0:T(8,128)S(1)}, f32[136,128]{1,0:T(8,128)S(1)}, u32[]{:S(2)}, u32[]{:S(2)}) collective-permute-start(f32[136,128]{1,0:T(8,128)S(1)} %get-tuple-element.63), channel_id=1, source_target_pairs={{0,24},{4,28},{8,16},{12,20},{16,8},{20,12},{24,0},{28,4},{32,56},... | collective-permute-start | bytes 208904 | tf_op jit(solution)/shard_map/ppermute | solution.py:436
  9.8 0.4 prep.1
  10.2 1.1 %local_attn.5 = (f32[1024,128]{1,0:T(8,128)S(1)}, bf16[1024,256]{1,0:T(8,128)(2,1)S(1)}) custom-call(bf16[1024,1024]{1,0:T(8,128)(2,1)S(1)} %copy-done, bf16[1024,1024]{1,0:T(8,128)(2,1)S(1)} %get-tuple-element.54.k_ref.refs_1_, bf16[1024,1024]{1,0:T(8,128)(2,1)S(1)} %get-tuple-element.55.v_ref.refs_2_, f32[8,1024]{1,0:T(8,128)S(1)} %get-tuple-element.64.refs_3_, ...), custom_call_target="tpu_custom_call" | custom-call | flops 201326592 | bytes 1310720 | tf_op jit(solution)/shard_map/local_attn/pallas_call | solution.py:374
  11.5 1.6 %collective-permute-done.3.refs_2_.refs_4_ = f32[136,128]{1,0:T(8,128)S(1)} collective-permute-done((f32[136,128]{1,0:T(8,128)S(1)}, f32[136,128]{1,0:T(8,128)S(1)}, u32[]{:S(2)}, u32[]{:S(2)}) %collective-permute-start.3) | collective-permute-done | bytes 69664 | tf_op jit(solution)/shard_map/ppermute | solution.py:436
  13.0 1.7 %collective-permute-done.4.refs_3_.refs_5_ = f32[136,128]{1,0:T(8,128)S(1)} collective-permute-done((f32[136,128]{1,0:T(8,128)S(1)}, f32[136,128]{1,0:T(8,128)S(1)}, u32[]{:S(2)}, u32[]{:S(2)}) %collective-permute-start.4) | collective-permute-done | bytes 69664 | tf_op jit(solution)/shard_map/ppermute | solution.py:436
  15.1 2.1 %local_attn.6 = (f32[1024,128]{1,0:T(8,128)S(1)}, f32[1024,128]{1,0:T(8,128)S(1)}, bf16[1024,256]{1,0:T(8,128)(2,1)S(1)}, bf16[1024,256]{1,0:T(8,128)(2,1)S(1)}) custom-call(bf16[1024,1024]{1,0:T(8,128)(2,1)S(1)} %copy-done, bf16[1024,1024]{1,0:T(8,128)(2,1)S(1)} %get-tuple-element.54.k_ref.refs_1_, bf16[1024,1024]{1,0:T(8,128)(2,1)S(1)} %get-tuple-element.55.v_ref.refs_2_, ...), custom_call_target="tpu_custom_call" | custom-call | flops 402653184 | bytes 2621440 | tf_op jit(solution)/shard_map/local_attn/pallas_call | solution.py:374
  17.1 2.1 %collective-permute-done.5.refs_1_ = f32[136,128]{1,0:T(8,128)S(1)} collective-permute-done((f32[136,128]{1,0:T(8,128)S(1)}, f32[136,128]{1,0:T(8,128)S(1)}, u32[]{:S(2)}, u32[]{:S(2)}) %collective-permute-start.5) | collective-permute-done | bytes 69664 | tf_op jit(solution)/shard_map/ppermute | solution.py:436
  19.3 3.4 %collective-permute-start.6 = (f32[136,128]{1,0:T(8,128)S(1)}, f32[136,128]{1,0:T(8,128)S(1)}, u32[]{:S(2)}, u32[]{:S(2)}) collective-permute-start(f32[136,128]{1,0:T(8,128)S(1)} %get-tuple-element.69.refs_5_.refs_0_), channel_id=1, source_target_pairs={{0,64},{4,68},{8,72},{12,76},{16,80},{20,84},{24,88},{28,92},{32,9... | collective-permute-start | bytes 208904 | tf_op jit(solution)/shard_map/ppermute | solution.py:436
  22.6 1.6 %collective-permute-start.1 = (f32[8,128]{1,0:T(8,128)S(1)}, f32[8,128]{1,0:T(8,128)S(1)}, u32[]{:S(2)}, u32[]{:S(2)}) collective-permute-start(f32[8,128]{1,0:T(8,128)S(1)} %get-tuple-element.59.refs_0_), channel_id=1, source_target_pairs={{0,1},{1,0},{2,3},{3,2},{4,5},{5,4},{6,7},{7,6},{8,9},{9,8},{10,11... | collective-permute-start | bytes 12296 | tf_op jit(solution)/shard_map/ppermute | solution.py:439
  24.2 2.1 %local_attn.7 = (f32[1024,128]{1,0:T(8,128)S(1)}, f32[1024,128]{1,0:T(8,128)S(1)}, bf16[1024,256]{1,0:T(8,128)(2,1)S(1)}, bf16[1024,256]{1,0:T(8,128)(2,1)S(1)}) custom-call(bf16[1024,1024]{1,0:T(8,128)(2,1)S(1)} %copy-done, bf16[1024,1024]{1,0:T(8,128)(2,1)S(1)} %get-tuple-element.54.k_ref.refs_1_, bf16[1024,1024]{1,0:T(8,128)(2,1)S(1)} %get-tuple-element.55.v_ref.refs_2_, ...), custom_call_target="tpu_custom_call" | custom-call | flops 402653184 | bytes 2621440 | tf_op jit(solution)/shard_map/local_attn/pallas_call | solution.py:374
  26.4 4.7 %collective-permute-start.7 = (f32[136,128]{1,0:T(8,128)S(1)}, f32[136,128]{1,0:T(8,128)S(1)}, u32[]{:S(2)}, u32[]{:S(2)}) collective-permute-start(f32[136,128]{1,0:T(8,128)S(1)} %get-tuple-element.73.refs_5_.refs_0_), channel_id=1, source_target_pairs={{0,192},{4,196},{8,200},{12,204},{16,208},{20,212},{24,216},{28,22... | collective-permute-start | bytes 208904 | tf_op jit(solution)/shard_map/ppermute | solution.py:436
  31.0 2.1 %local_attn.8 = (f32[1024,128]{1,0:T(8,128)S(1)}, f32[1024,128]{1,0:T(8,128)S(1)}, bf16[1024,256]{1,0:T(8,128)(2,1)S(1)}, bf16[1024,256]{1,0:T(8,128)(2,1)S(1)}) custom-call(bf16[1024,1024]{1,0:T(8,128)(2,1)S(1)} %copy-done, bf16[1024,1024]{1,0:T(8,128)(2,1)S(1)} %get-tuple-element.54.k_ref.refs_1_, bf16[1024,1024]{1,0:T(8,128)(2,1)S(1)} %get-tuple-element.55.v_ref.refs_2_, ...), custom_call_target="tpu_custom_call" | custom-call | flops 402653184 | bytes 2621440 | tf_op jit(solution)/shard_map/local_attn/pallas_call | solution.py:374
  33.1 0.8 %collective-permute-done.7.refs_1_ = f32[136,128]{1,0:T(8,128)S(1)} collective-permute-done((f32[136,128]{1,0:T(8,128)S(1)}, f32[136,128]{1,0:T(8,128)S(1)}, u32[]{:S(2)}, u32[]{:S(2)}) %collective-permute-start.7) | collective-permute-done | bytes 69664 | tf_op jit(solution)/shard_map/ppermute | solution.py:436
  34.0 1.2 %collective-permute-start.9 = (f32[256,128]{1,0:T(8,128)S(1)}, f32[256,128]{1,0:T(8,128)S(1)}, u32[]{:S(2)}, u32[]{:S(2)}) collective-permute-start(f32[256,128]{1,0:T(8,128)S(1)} %get-tuple-element.80), channel_id=1, source_target_pairs={{0,16},{4,20},{8,24},{12,28},{16,0},{20,4},{24,8},{28,12},{32,48},... | collective-permute-start | bytes 393224 | tf_op jit(solution)/shard_map/ppermute | solution.py:436
  35.2 0.7 %collective-permute-start.10 = (f32[256,128]{1,0:T(8,128)S(1)}, f32[256,128]{1,0:T(8,128)S(1)}, u32[]{:S(2)}, u32[]{:S(2)}) collective-permute-start(f32[256,128]{1,0:T(8,128)S(1)} %get-tuple-element.81), channel_id=1, source_target_pairs={{0,8},{4,12},{8,0},{12,4},{16,24},{20,28},{24,16},{28,20},{32,40},... | collective-permute-start | bytes 393224 | tf_op jit(solution)/shard_map/ppermute | solution.py:436
  35.9 2.3 %collective-permute-start.11 = (f32[256,128]{1,0:T(8,128)S(1)}, f32[256,128]{1,0:T(8,128)S(1)}, u32[]{:S(2)}, u32[]{:S(2)}) collective-permute-start(f32[256,128]{1,0:T(8,128)S(1)} %get-tuple-element.82), channel_id=1, source_target_pairs={{0,24},{4,28},{8,16},{12,20},{16,8},{20,12},{24,0},{28,4},{32,56},... | collective-permute-start | bytes 393224 | tf_op jit(solution)/shard_map/ppermute | solution.py:436
  38.2 3.0 %collective-permute-start.8 = (f32[8,128]{1,0:T(8,128)S(1)}, f32[8,128]{1,0:T(8,128)S(1)}, u32[]{:S(2)}, u32[]{:S(2)}) collective-permute-start(f32[8,128]{1,0:T(8,128)S(1)} %want.1.refs_0_), channel_id=1, source_target_pairs={{0,3},{1,2},{2,1},{3,0},{4,7},{5,6},{6,5},{7,4},{8,11},{9,10},{10,... | collective-permute-start | bytes 12296 | tf_op jit(solution)/shard_map/ppermute | solution.py:439
  41.2 1.1 %local_attn.9 = (f32[1024,128]{1,0:T(8,128)S(1)}, bf16[1024,256]{1,0:T(8,128)(2,1)S(1)}) custom-call(bf16[1024,1024]{1,0:T(8,128)(2,1)S(1)} %copy-done, bf16[1024,1024]{1,0:T(8,128)(2,1)S(1)} %get-tuple-element.54.k_ref.refs_1_, bf16[1024,1024]{1,0:T(8,128)(2,1)S(1)} %get-tuple-element.55.v_ref.refs_2_, f32[8,1024]{1,0:T(8,128)S(1)} %get-tuple-element.64.refs_3_, ...), custom_call_target="tpu_custom_call" | custom-call | flops 201326592 | bytes 1310720 | tf_op jit(solution)/shard_map/local_attn/pallas_call | solution.py:374
  42.3 0.7 %collective-permute-done.8.refs_1_ = f32[8,128]{1,0:T(8,128)S(1)} collective-permute-done((f32[8,128]{1,0:T(8,128)S(1)}, f32[8,128]{1,0:T(8,128)S(1)}, u32[]{:S(2)}, u32[]{:S(2)}) %collective-permute-start.8) | collective-permute-done | bytes 4128 | tf_op jit(solution)/shard_map/ppermute | solution.py:439
  43.0 0.4 spread.1
  43.5 1.4 %last.3 = (bf16[1024,1024]{1,0:T(8,128)(2,1)}, f32[8,128]{1,0:T(8,128)S(1)}) custom-call(f32[1,1024]{1,0:T(1,128)S(1)} %bitcast.1, f32[4,128,128]{2,1,0:T(8,128)S(1)} %get-tuple-element.89.p_ref, f32[1024,128]{1,0:T(8,128)S(1)} %get-tuple-element.66.refs_4_.rest_0_, f32[1024,128]{1,0:T(8,128)S(1)} %get-tuple-element.67.refs_2_.rest_1_, ...), custom_call_target="tpu_custom_call" | custom-call | flops 201326592 | bytes 2621440 | tf_op jit(solution)/shard_map/last/pallas_call | solution.py:418
  45.0 0.6 %collective-permute-start.13 = (f32[2,16,128]{2,1,0:T(8,128)S(1)}, f32[2,16,128]{2,1,0:T(8,128)S(1)}, u32[]{:S(2)}, u32[]{:S(2)}) collective-permute-start(f32[2,16,128]{2,1,0:T(8,128)S(1)} %get-tuple-element.99), channel_id=1, source_target_pairs={{0,1},{1,0},{2,3},{3,2},{4,5},{5,4},{6,7},{7,6},{8,9},{9,8},{10,11... | collective-permute-start | bytes 49160 | tf_op jit(solution)/shard_map/ppermute | solution.py:439
  45.6 1.4 %last.4 = (bf16[1024,1024]{1,0:T(8,128)(2,1)}, f32[8,128]{1,0:T(8,128)S(1)}) custom-call(f32[1,1024]{1,0:T(1,128)S(1)} %bitcast.2, f32[4,128,128]{2,1,0:T(8,128)S(1)} %get-tuple-element.89.p_ref, f32[1024,128]{1,0:T(8,128)S(1)} %get-tuple-element.68.refs_3_.rest_0_, ...), custom_call_target="tpu_custom_call", output_to_operand_aliasing={{0}: (6, {})} | custom-call | flops 201326592 | bytes 2621440 | tf_op jit(solution)/shard_map/last/pallas_call | solution.py:418
  47.1 1.7 %collective-permute-done.13.refs_0_ = f32[2,16,128]{2,1,0:T(8,128)S(1)} collective-permute-done((f32[2,16,128]{2,1,0:T(8,128)S(1)}, f32[2,16,128]{2,1,0:T(8,128)S(1)}, u32[]{:S(2)}, u32[]{:S(2)}) %collective-permute-start.13) | collective-permute-done | bytes 16416 | tf_op jit(solution)/shard_map/ppermute | solution.py:439
  48.8 3.0 %collective-permute-start.14 = (f32[16,128]{1,0:T(8,128)S(1)}, f32[16,128]{1,0:T(8,128)S(1)}, u32[]{:S(2)}, u32[]{:S(2)}) collective-permute-start(f32[16,128]{1,0:T(8,128)S(1)} %get-tuple-element.104), channel_id=1, source_target_pairs={{0,3},{1,2},{2,1},{3,0},{4,7},{5,6},{6,5},{7,4},{8,11},{9,10},{10,... | collective-permute-start | bytes 24584 | tf_op jit(solution)/shard_map/ppermute | solution.py:439
  51.8 2.0 %last.5 = (bf16[1024,1024]{1,0:T(8,128)(2,1)}, f32[8,128]{1,0:T(8,128)S(1)}) custom-call(f32[1,1024]{1,0:T(1,128)S(1)} %bitcast.3, f32[4,144,128]{2,1,0:T(8,128)S(1)} %collective-permute-done.12.refs_1_.p_ref, f32[1024,128]{1,0:T(8,128)S(1)} %get-tuple-element.72.refs_4_.rest_0_, ...), custom_call_target="tpu_custom_call", output_to_operand_aliasing={{0}: (10, {})} | custom-call | flops 402653184 | bytes 5242880 | tf_op jit(solution)/shard_map/last/pallas_call | solution.py:418
  53.8 0.6 %sum.1 = f32[16,128]{1,0:T(8,128)} custom-call(f32[16,128]{1,0:T(8,128)S(1)} %get-tuple-element.102.rest_9_.refs_0_, f32[16,128]{1,0:T(8,128)S(1)} %collective-permute-done.14.refs_1_, f32[8,128]{1,0:T(8,128)S(1)} %get-tuple-element.105.refs_2_), custom_call_target="tpu_custom_call" | custom-call | tf_op jit(solution)/shard_map/sum/pallas_call | solution.py:301
  (26 shorter events, 1.0 us)
Async XLA Ops:
  3.9 1.6 %collective-permute-start = (f32[4,136,128]{2,1,0:T(8,128)S(1)}, f32[4,136,128]{2,1,0:T(8,128)S(1)}, u32[]{:S(2)}, u32[]{:S(2)}) collective-permute-start(f32[4,136,128]{2,1,0:T(8,128)S(1)} %get-tuple-element.58), channel_id=1, source_target_pairs={{0,4},{4,0},{8,12},{12,8},{16,20},{20,16},{24,28},{28,24},{32,36},... | collective-permute-start | bytes 835592 | tf_op jit(solution)/shard_map/ppermute | solution.py:436
  4.0 5.9 %copy-start.1 = (f32[8,1024]{1,0:T(8,128)S(1)}, f32[8,1024]{1,0:T(8,128)}, u32[]{:S(2)}) copy-start(f32[8,1024]{1,0:T(8,128)} %refs_0_.6) | copy-start | bytes 98308
  4.0 6.2 %copy-start = (bf16[1024,1024]{1,0:T(8,128)(2,1)S(1)}, bf16[1024,1024]{1,0:T(8,128)(2,1)}, u32[]{:S(2)}) copy-start(bf16[1024,1024]{1,0:T(8,128)(2,1)} %refs_0_.11) | copy-start | bytes 6291460
  5.6 5.9 %collective-permute-start.2 = (f32[136,128]{1,0:T(8,128)S(1)}, f32[136,128]{1,0:T(8,128)S(1)}, u32[]{:S(2)}, u32[]{:S(2)}) collective-permute-start(f32[136,128]{1,0:T(8,128)S(1)} %get-tuple-element.61), channel_id=1, source_target_pairs={{0,16},{4,20},{8,24},{12,28},{16,0},{20,4},{24,8},{28,12},{32,48},... | collective-permute-start | bytes 208904 | tf_op jit(solution)/shard_map/ppermute | solution.py:436
  8.7 4.4 %collective-permute-start.3 = (f32[136,128]{1,0:T(8,128)S(1)}, f32[136,128]{1,0:T(8,128)S(1)}, u32[]{:S(2)}, u32[]{:S(2)}) collective-permute-start(f32[136,128]{1,0:T(8,128)S(1)} %get-tuple-element.62), channel_id=1, source_target_pairs={{0,8},{4,12},{8,0},{12,4},{16,24},{20,28},{24,16},{28,20},{32,40},... | collective-permute-start | bytes 208904 | tf_op jit(solution)/shard_map/ppermute | solution.py:436
  9.3 5.5 %collective-permute-start.4 = (f32[136,128]{1,0:T(8,128)S(1)}, f32[136,128]{1,0:T(8,128)S(1)}, u32[]{:S(2)}, u32[]{:S(2)}) collective-permute-start(f32[136,128]{1,0:T(8,128)S(1)} %get-tuple-element.63), channel_id=1, source_target_pairs={{0,24},{4,28},{8,16},{12,20},{16,8},{20,12},{24,0},{28,4},{32,56},... | collective-permute-start | bytes 208904 | tf_op jit(solution)/shard_map/ppermute | solution.py:436
  14.9 4.4 %collective-permute-start.5 = (f32[136,128]{1,0:T(8,128)S(1)}, f32[136,128]{1,0:T(8,128)S(1)}, u32[]{:S(2)}, u32[]{:S(2)}) collective-permute-start(f32[136,128]{1,0:T(8,128)S(1)} %slab.1.refs_5_.refs_0_), channel_id=1, source_target_pairs={{0,32},{4,36},{8,40},{12,44},{16,48},{20,52},{24,56},{28,60},{32,0... | collective-permute-start | bytes 208904 | tf_op jit(solution)/shard_map/ppermute | solution.py:436
  19.3 7.0 %collective-permute-start.6 = (f32[136,128]{1,0:T(8,128)S(1)}, f32[136,128]{1,0:T(8,128)S(1)}, u32[]{:S(2)}, u32[]{:S(2)}) collective-permute-start(f32[136,128]{1,0:T(8,128)S(1)} %get-tuple-element.69.refs_5_.refs_0_), channel_id=1, source_target_pairs={{0,64},{4,68},{8,72},{12,76},{16,80},{20,84},{24,88},{28,92},{32,9... | collective-permute-start | bytes 208904 | tf_op jit(solution)/shard_map/ppermute | solution.py:436
  22.6 3.7 %collective-permute-start.1 = (f32[8,128]{1,0:T(8,128)S(1)}, f32[8,128]{1,0:T(8,128)S(1)}, u32[]{:S(2)}, u32[]{:S(2)}) collective-permute-start(f32[8,128]{1,0:T(8,128)S(1)} %get-tuple-element.59.refs_0_), channel_id=1, source_target_pairs={{0,1},{1,0},{2,3},{3,2},{4,5},{5,4},{6,7},{7,6},{8,9},{9,8},{10,11... | collective-permute-start | bytes 12296 | tf_op jit(solution)/shard_map/ppermute | solution.py:439
  26.4 7.5 %collective-permute-start.7 = (f32[136,128]{1,0:T(8,128)S(1)}, f32[136,128]{1,0:T(8,128)S(1)}, u32[]{:S(2)}, u32[]{:S(2)}) collective-permute-start(f32[136,128]{1,0:T(8,128)S(1)} %get-tuple-element.73.refs_5_.refs_0_), channel_id=1, source_target_pairs={{0,192},{4,196},{8,200},{12,204},{16,208},{20,212},{24,216},{28,22... | collective-permute-start | bytes 208904 | tf_op jit(solution)/shard_map/ppermute | solution.py:436
  34.0 9.0 %collective-permute-start.9 = (f32[256,128]{1,0:T(8,128)S(1)}, f32[256,128]{1,0:T(8,128)S(1)}, u32[]{:S(2)}, u32[]{:S(2)}) collective-permute-start(f32[256,128]{1,0:T(8,128)S(1)} %get-tuple-element.80), channel_id=1, source_target_pairs={{0,16},{4,20},{8,24},{12,28},{16,0},{20,4},{24,8},{28,12},{32,48},... | collective-permute-start | bytes 393224 | tf_op jit(solution)/shard_map/ppermute | solution.py:436
  35.2 7.8 %collective-permute-start.10 = (f32[256,128]{1,0:T(8,128)S(1)}, f32[256,128]{1,0:T(8,128)S(1)}, u32[]{:S(2)}, u32[]{:S(2)}) collective-permute-start(f32[256,128]{1,0:T(8,128)S(1)} %get-tuple-element.81), channel_id=1, source_target_pairs={{0,8},{4,12},{8,0},{12,4},{16,24},{20,28},{24,16},{28,20},{32,40},... | collective-permute-start | bytes 393224 | tf_op jit(solution)/shard_map/ppermute | solution.py:436
  35.9 7.1 %collective-permute-start.11 = (f32[256,128]{1,0:T(8,128)S(1)}, f32[256,128]{1,0:T(8,128)S(1)}, u32[]{:S(2)}, u32[]{:S(2)}) collective-permute-start(f32[256,128]{1,0:T(8,128)S(1)} %get-tuple-element.82), channel_id=1, source_target_pairs={{0,24},{4,28},{8,16},{12,20},{16,8},{20,12},{24,0},{28,4},{32,56},... | collective-permute-start | bytes 393224 | tf_op jit(solution)/shard_map/ppermute | solution.py:436
  38.2 5.3 %copy-start.2 = (f32[1024]{0:T(1024)S(1)}, f32[1024]{0:T(1024)}, u32[]{:S(2)}) copy-start(f32[1024]{0:T(1024)} %param.10) | copy-start | bytes 12292
  38.2 4.8 %collective-permute-start.8 = (f32[8,128]{1,0:T(8,128)S(1)}, f32[8,128]{1,0:T(8,128)S(1)}, u32[]{:S(2)}, u32[]{:S(2)}) collective-permute-start(f32[8,128]{1,0:T(8,128)S(1)} %want.1.refs_0_), channel_id=1, source_target_pairs={{0,3},{1,2},{2,1},{3,0},{4,7},{5,6},{6,5},{7,4},{8,11},{9,10},{10,... | collective-permute-start | bytes 12296 | tf_op jit(solution)/shard_map/ppermute | solution.py:439
  43.4 1.7 %collective-permute-start.12 = (f32[4,144,128]{2,1,0:T(8,128)S(1)}, f32[4,144,128]{2,1,0:T(8,128)S(1)}, u32[]{:S(2)}, u32[]{:S(2)}) collective-permute-start(f32[4,144,128]{2,1,0:T(8,128)S(1)} %get-tuple-element.84), channel_id=1, source_target_pairs={{0,4},{4,0},{8,12},{12,8},{16,20},{20,16},{24,28},{28,24},{32,36},... | collective-permute-start | bytes 884744 | tf_op jit(solution)/shard_map/ppermute | solution.py:436
  45.0 3.7 %collective-permute-start.13 = (f32[2,16,128]{2,1,0:T(8,128)S(1)}, f32[2,16,128]{2,1,0:T(8,128)S(1)}, u32[]{:S(2)}, u32[]{:S(2)}) collective-permute-start(f32[2,16,128]{2,1,0:T(8,128)S(1)} %get-tuple-element.99), channel_id=1, source_target_pairs={{0,1},{1,0},{2,3},{3,2},{4,5},{5,4},{6,7},{7,6},{8,9},{9,8},{10,11... | collective-permute-start | bytes 49160 | tf_op jit(solution)/shard_map/ppermute | solution.py:439
  48.8 5.0 %collective-permute-start.14 = (f32[16,128]{1,0:T(8,128)S(1)}, f32[16,128]{1,0:T(8,128)S(1)}, u32[]{:S(2)}, u32[]{:S(2)}) collective-permute-start(f32[16,128]{1,0:T(8,128)S(1)} %get-tuple-element.104), channel_id=1, source_target_pairs={{0,3},{1,2},{2,1},{3,0},{4,7},{5,6},{6,5},{7,4},{8,11},{9,10},{10,... | collective-permute-start | bytes 24584 | tf_op jit(solution)/shard_map/ppermute | solution.py:439

commit v4 on v3

--- a/solution.py
+++ b/solution.py
@@ -445,8 +445,8 @@
     send, keep, k_heads, v_heads = summaries(keys, values, log_decay, decode_map)
     recv = swap(send, 1)
 
-    *t, want = small(pair_kernel, [ext] * 4 + [(8, 128)], "pair")(keep, recv)
-    cr, ct = small(prep_kernel, [(heads, tokens), (tokens, heads)], "prep", (t[0],))(log_decay)
+    cr, ct = small(prep_kernel, [(heads, tokens), (tokens, heads)], "prep", (keep,))(log_decay)
+    *t, want = small(pair_kernel, [ext] * 4 + [(8, 128)], "pair", (cr,))(keep, recv)
     attn, scaled = [None] * heads, [None] * heads
 
     def local(which, *after):
@@ -479,10 +479,9 @@
     other = swap(other, 1)
 
     gain = out_gain.reshape(1, -1)
-    out, mark = last_part((0, 1), gain, own, attn, scaled)
-    slot_send, near, far = small(merge_kernel, [(2, 16, 128), (16, 128), (16, 128)], "merge", (mark,))(slots, other)
+    slot_send, near, far = small(merge_kernel, [(2, 16, 128), (16, 128), (16, 128)], "merge")(slots, other)
     got = swap_y(slot_send, 1)
-    out, mark = last_part((2, 3), gain, own, attn, scaled, out, (near,))
+    out, mark = last_part((0, 1, 2, 3), gain, own, attn, scaled, None, (near,))
     near, far = small(slots_kernel, [(16, 128)] * 2, "slots", (mark,))(got, near, far)
     got = swap_y(far, 3)
     out, mark = last_part((4, 5, 6, 7), gain, other, attn, scaled, out, (near,))

time: 54.5 us -> 54.5 us (level)
  Pallas kernels: 18.4 us -> 17.6 us
  waiting for transfers between devices: 9.42 us -> 10.2 us
    ppermute x11, waiting for transfers between devices: 7 us -> 8.39 us  [swap(): return lax.ppermute(a, 'ctx', [(i, i ^ mask) for i in range(ctx_size)])]
    pallas_call x3 -> x2, Pallas kernels: 4.79 us -> 3.95 us  [last_part(): pl.pallas_call(functools.partial(last_kernel, heads), out_shape=[jax.Shap...]
    ppermute x4, waiting for transfers between devices: 2.42 us -> 1.79 us  [swap_y(): return lax.ppermute(a, 'head', [(i, i ^ mask) for i in range(head_size)])]
  transfers between devices with their start and end apart: 15 -> 15, of which waited for: 9 -> 9; matrix products, arithmetic and copies ran while one was open for 0% -> 0% of each run, Pallas kernels for 27% -> 25%
where the time goes in v4:
time: 54.5 us; the launch traced here: 54.4 us
  starting transfers between devices  25.1 us (46%)
  Pallas kernels  17.6 us (32%)
  waiting for transfers between devices  10.2 us (19%)
  between operations  1.46 us (3%)
    ppermute x11, starting transfers between devices, swap(): return lax.ppermute(a, 'ctx', [(i, i ^ mask) for i in range(ctx_size)])  16.9 us
    pallas_call x5, Pallas kernels, local_part(): pl.pallas_call(body, out_shape=[jax.ShapeDtypeStruct((tokens, 128), f32)]...  8.45 us
    ppermute x11, waiting for transfers between devices, swap(): return lax.ppermute(a, 'ctx', [(i, i ^ mask) for i in range(ctx_size)])  8.39 us
    ppermute x4, starting transfers between devices, swap_y(): return lax.ppermute(a, 'head', [(i, i ^ mask) for i in range(head_size)])  8.25 us
    pallas_call x2, Pallas kernels, last_part(): pl.pallas_call(functools.partial(last_kernel, heads), out_shape=[jax.Shap...  3.95 us
    pallas_call x1, Pallas kernels, summaries(): pl.pallas_call(send_kernel, out_shape=[out, jax.ShapeDtypeStruct((heads,...  2.59 us
    ppermute x4, waiting for transfers between devices, swap_y(): return lax.ppermute(a, 'head', [(i, i ^ mask) for i in range(head_size)])  1.79 us
    pallas_call x12, Pallas kernels, call(): pl.pallas_call(body, out_shape=[jax.ShapeDtypeStruct(s, f32) for s in out...  1.62 us
  transfers between devices with their start and end apart: 15, of which 9 were waited for; matrix products, arithmetic and copies ran while one was open for 0% of the time, Pallas kernels for 25%

profile of v4, /device:TPU:32, one launch (start us, length us, event | category | flops | bytes accessed | tf_op | source)
XLA Modules:
  0.0 54.4 jit_solution(17402515933753845905)
XLA Ops:
  1.3 2.6 %summary_send.1 = (f32[4,136,128]{2,1,0:T(8,128)S(1)}, f32[8,1024]{1,0:T(8,128)S(1)}, f32[16,128]{1,0:T(8,128)S(1)}, bf16[1024,1024]{1,0:T(8,128)(2,1)S(1)}, bf16[1024,1024]{1,0:T(8,128)(2,1)S(1)}) custom-call(bf16[1024,1024]{1,0:T(8,128)(2,1)} %k_hbm.1, bf16[1024,1024]{1,0:T(8,128)(2,1)} %v_hbm.1, f32[8,1024]{1,0:T(8,128)} %refs_0_.6, s32[1]{0:T(128)S(6)} %copy.10.map_ref), custom_call_target="tpu_custom_call" | custom-call | flops 268435456 | bytes 2097152 | tf_op jit(solution)/shard_map/summary_send/pallas_call | solution.py:140
  4.0 1.0 %summary_keep.1.refs_1_.refs_0_.refs_6_ = f32[4,136,128]{2,1,0:T(8,128)S(1)} custom-call(bf16[1024,1024]{1,0:T(8,128)(2,1)S(1)} %get-tuple-element.52.k_ref.refs_1_, bf16[1024,1024]{1,0:T(8,128)(2,1)S(1)} %get-tuple-element.53.v_ref.refs_2_, f32[8,1024]{1,0:T(8,128)S(1)} %get-tuple-element.54.w_ref, f32[16,128]{1,0:T(8,128)S(1)} %get-tuple-element.55.tot_ref), custom_call_target="tpu_custom_call" | custom-call | flops 268435456 | bytes 2097152 | tf_op jit(solution)/shard_map/summary_keep/pallas_call | solution.py:160
  5.0 0.4 prep.1
  5.6 3.1 %collective-permute-start.2 = (f32[136,128]{1,0:T(8,128)S(1)}, f32[136,128]{1,0:T(8,128)S(1)}, u32[]{:S(2)}, u32[]{:S(2)}) collective-permute-start(f32[136,128]{1,0:T(8,128)S(1)} %get-tuple-element.60), channel_id=1, source_target_pairs={{0,16},{4,20},{8,24},{12,28},{16,0},{20,4},{24,8},{28,12},{32,48},... | collective-permute-start | bytes 208904 | tf_op jit(solution)/shard_map/ppermute | solution.py:436
  8.7 0.6 %collective-permute-start.3 = (f32[136,128]{1,0:T(8,128)S(1)}, f32[136,128]{1,0:T(8,128)S(1)}, u32[]{:S(2)}, u32[]{:S(2)}) collective-permute-start(f32[136,128]{1,0:T(8,128)S(1)} %get-tuple-element.61), channel_id=1, source_target_pairs={{0,8},{4,12},{8,0},{12,4},{16,24},{20,28},{24,16},{28,20},{32,40},... | collective-permute-start | bytes 208904 | tf_op jit(solution)/shard_map/ppermute | solution.py:436
  9.3 0.6 %collective-permute-start.4 = (f32[136,128]{1,0:T(8,128)S(1)}, f32[136,128]{1,0:T(8,128)S(1)}, u32[]{:S(2)}, u32[]{:S(2)}) collective-permute-start(f32[136,128]{1,0:T(8,128)S(1)} %get-tuple-element.62), channel_id=1, source_target_pairs={{0,24},{4,28},{8,16},{12,20},{16,8},{20,12},{24,0},{28,4},{32,56},... | collective-permute-start | bytes 208904 | tf_op jit(solution)/shard_map/ppermute | solution.py:436
  9.8 1.1 %local_attn.5 = (f32[1024,128]{1,0:T(8,128)S(1)}, bf16[1024,256]{1,0:T(8,128)(2,1)S(1)}) custom-call(bf16[1024,1024]{1,0:T(8,128)(2,1)S(1)} %copy-done, bf16[1024,1024]{1,0:T(8,128)(2,1)S(1)} %get-tuple-element.52.k_ref.refs_1_, bf16[1024,1024]{1,0:T(8,128)(2,1)S(1)} %get-tuple-element.53.v_ref.refs_2_, f32[8,1024]{1,0:T(8,128)S(1)} %get-tuple-element.57.refs_2_.refs_3_, ...), custom_call_target="tpu_custom_call" | custom-call | flops 201326592 | bytes 1310720 | tf_op jit(solution)/shard_map/local_attn/pallas_call | solution.py:374
  11.0 0.6 %collective-permute-done.2.refs_1_.refs_3_ = f32[136,128]{1,0:T(8,128)S(1)} collective-permute-done((f32[136,128]{1,0:T(8,128)S(1)}, f32[136,128]{1,0:T(8,128)S(1)}, u32[]{:S(2)}, u32[]{:S(2)}) %collective-permute-start.2) | collective-permute-done | bytes 69664 | tf_op jit(solution)/shard_map/ppermute | solution.py:436
  11.5 1.6 %collective-permute-done.3.refs_2_.refs_4_ = f32[136,128]{1,0:T(8,128)S(1)} collective-permute-done((f32[136,128]{1,0:T(8,128)S(1)}, f32[136,128]{1,0:T(8,128)S(1)}, u32[]{:S(2)}, u32[]{:S(2)}) %collective-permute-start.3) | collective-permute-done | bytes 69664 | tf_op jit(solution)/shard_map/ppermute | solution.py:436
  13.1 1.7 %collective-permute-done.4.refs_3_.refs_5_ = f32[136,128]{1,0:T(8,128)S(1)} collective-permute-done((f32[136,128]{1,0:T(8,128)S(1)}, f32[136,128]{1,0:T(8,128)S(1)}, u32[]{:S(2)}, u32[]{:S(2)}) %collective-permute-start.4) | collective-permute-done | bytes 69664 | tf_op jit(solution)/shard_map/ppermute | solution.py:436
  15.1 2.1 %local_attn.6 = (f32[1024,128]{1,0:T(8,128)S(1)}, f32[1024,128]{1,0:T(8,128)S(1)}, bf16[1024,256]{1,0:T(8,128)(2,1)S(1)}, bf16[1024,256]{1,0:T(8,128)(2,1)S(1)}) custom-call(bf16[1024,1024]{1,0:T(8,128)(2,1)S(1)} %copy-done, bf16[1024,1024]{1,0:T(8,128)(2,1)S(1)} %get-tuple-element.52.k_ref.refs_1_, bf16[1024,1024]{1,0:T(8,128)(2,1)S(1)} %get-tuple-element.53.v_ref.refs_2_, ...), custom_call_target="tpu_custom_call" | custom-call | flops 402653184 | bytes 2621440 | tf_op jit(solution)/shard_map/local_attn/pallas_call | solution.py:374
  17.2 2.0 %collective-permute-done.5.refs_1_ = f32[136,128]{1,0:T(8,128)S(1)} collective-permute-done((f32[136,128]{1,0:T(8,128)S(1)}, f32[136,128]{1,0:T(8,128)S(1)}, u32[]{:S(2)}, u32[]{:S(2)}) %collective-permute-start.5) | collective-permute-done | bytes 69664 | tf_op jit(solution)/shard_map/ppermute | solution.py:436
  19.3 3.4 %collective-permute-start.6 = (f32[136,128]{1,0:T(8,128)S(1)}, f32[136,128]{1,0:T(8,128)S(1)}, u32[]{:S(2)}, u32[]{:S(2)}) collective-permute-start(f32[136,128]{1,0:T(8,128)S(1)} %get-tuple-element.67.refs_5_.refs_0_), channel_id=1, source_target_pairs={{0,64},{4,68},{8,72},{12,76},{16,80},{20,84},{24,88},{28,92},{32,9... | collective-permute-start | bytes 208904 | tf_op jit(solution)/shard_map/ppermute | solution.py:436
  22.6 1.6 %collective-permute-start.1 = (f32[8,128]{1,0:T(8,128)S(1)}, f32[8,128]{1,0:T(8,128)S(1)}, u32[]{:S(2)}, u32[]{:S(2)}) collective-permute-start(f32[8,128]{1,0:T(8,128)S(1)} %get-tuple-element.58.refs_0_), channel_id=1, source_target_pairs={{0,1},{1,0},{2,3},{3,2},{4,5},{5,4},{6,7},{7,6},{8,9},{9,8},{10,11... | collective-permute-start | bytes 12296 | tf_op jit(solution)/shard_map/ppermute | solution.py:439
  24.2 2.1 %local_attn.7 = (f32[1024,128]{1,0:T(8,128)S(1)}, f32[1024,128]{1,0:T(8,128)S(1)}, bf16[1024,256]{1,0:T(8,128)(2,1)S(1)}, bf16[1024,256]{1,0:T(8,128)(2,1)S(1)}) custom-call(bf16[1024,1024]{1,0:T(8,128)(2,1)S(1)} %copy-done, bf16[1024,1024]{1,0:T(8,128)(2,1)S(1)} %get-tuple-element.52.k_ref.refs_1_, bf16[1024,1024]{1,0:T(8,128)(2,1)S(1)} %get-tuple-element.53.v_ref.refs_2_, ...), custom_call_target="tpu_custom_call" | custom-call | flops 402653184 | bytes 2621440 | tf_op jit(solution)/shard_map/local_attn/pallas_call | solution.py:374
  26.4 4.7 %collective-permute-start.7 = (f32[136,128]{1,0:T(8,128)S(1)}, f32[136,128]{1,0:T(8,128)S(1)}, u32[]{:S(2)}, u32[]{:S(2)}) collective-permute-start(f32[136,128]{1,0:T(8,128)S(1)} %get-tuple-element.71.refs_5_.refs_0_), channel_id=1, source_target_pairs={{0,192},{4,196},{8,200},{12,204},{16,208},{20,212},{24,216},{28,22... | collective-permute-start | bytes 208904 | tf_op jit(solution)/shard_map/ppermute | solution.py:436
  31.0 2.1 %local_attn.8 = (f32[1024,128]{1,0:T(8,128)S(1)}, f32[1024,128]{1,0:T(8,128)S(1)}, bf16[1024,256]{1,0:T(8,128)(2,1)S(1)}, bf16[1024,256]{1,0:T(8,128)(2,1)S(1)}) custom-call(bf16[1024,1024]{1,0:T(8,128)(2,1)S(1)} %copy-done, bf16[1024,1024]{1,0:T(8,128)(2,1)S(1)} %get-tuple-element.52.k_ref.refs_1_, bf16[1024,1024]{1,0:T(8,128)(2,1)S(1)} %get-tuple-element.53.v_ref.refs_2_, ...), custom_call_target="tpu_custom_call" | custom-call | flops 402653184 | bytes 2621440 | tf_op jit(solution)/shard_map/local_attn/pallas_call | solution.py:374
  33.1 0.8 %collective-permute-done.7.refs_1_ = f32[136,128]{1,0:T(8,128)S(1)} collective-permute-done((f32[136,128]{1,0:T(8,128)S(1)}, f32[136,128]{1,0:T(8,128)S(1)}, u32[]{:S(2)}, u32[]{:S(2)}) %collective-permute-start.7) | collective-permute-done | bytes 69664 | tf_op jit(solution)/shard_map/ppermute | solution.py:436
  34.0 1.3 %collective-permute-start.9 = (f32[256,128]{1,0:T(8,128)S(1)}, f32[256,128]{1,0:T(8,128)S(1)}, u32[]{:S(2)}, u32[]{:S(2)}) collective-permute-start(f32[256,128]{1,0:T(8,128)S(1)} %get-tuple-element.78), channel_id=1, source_target_pairs={{0,16},{4,20},{8,24},{12,28},{16,0},{20,4},{24,8},{28,12},{32,48},... | collective-permute-start | bytes 393224 | tf_op jit(solution)/shard_map/ppermute | solution.py:436
  35.3 0.6 %collective-permute-start.10 = (f32[256,128]{1,0:T(8,128)S(1)}, f32[256,128]{1,0:T(8,128)S(1)}, u32[]{:S(2)}, u32[]{:S(2)}) collective-permute-start(f32[256,128]{1,0:T(8,128)S(1)} %get-tuple-element.79), channel_id=1, source_target_pairs={{0,8},{4,12},{8,0},{12,4},{16,24},{20,28},{24,16},{28,20},{32,40},... | collective-permute-start | bytes 393224 | tf_op jit(solution)/shard_map/ppermute | solution.py:436
  35.9 2.2 %collective-permute-start.11 = (f32[256,128]{1,0:T(8,128)S(1)}, f32[256,128]{1,0:T(8,128)S(1)}, u32[]{:S(2)}, u32[]{:S(2)}) collective-permute-start(f32[256,128]{1,0:T(8,128)S(1)} %get-tuple-element.80), channel_id=1, source_target_pairs={{0,24},{4,28},{8,16},{12,20},{16,8},{20,12},{24,0},{28,4},{32,56},... | collective-permute-start | bytes 393224 | tf_op jit(solution)/shard_map/ppermute | solution.py:436
  38.2 3.0 %collective-permute-start.8 = (f32[8,128]{1,0:T(8,128)S(1)}, f32[8,128]{1,0:T(8,128)S(1)}, u32[]{:S(2)}, u32[]{:S(2)}) collective-permute-start(f32[8,128]{1,0:T(8,128)S(1)} %want.1.refs_0_), channel_id=1, source_target_pairs={{0,3},{1,2},{2,1},{3,0},{4,7},{5,6},{6,5},{7,4},{8,11},{9,10},{10,... | collective-permute-start | bytes 12296 | tf_op jit(solution)/shard_map/ppermute | solution.py:439
  41.2 1.1 %local_attn.9 = (f32[1024,128]{1,0:T(8,128)S(1)}, bf16[1024,256]{1,0:T(8,128)(2,1)S(1)}) custom-call(bf16[1024,1024]{1,0:T(8,128)(2,1)S(1)} %copy-done, bf16[1024,1024]{1,0:T(8,128)(2,1)S(1)} %get-tuple-element.52.k_ref.refs_1_, bf16[1024,1024]{1,0:T(8,128)(2,1)S(1)} %get-tuple-element.53.v_ref.refs_2_, f32[8,1024]{1,0:T(8,128)S(1)} %get-tuple-element.57.refs_2_.refs_3_, ...), custom_call_target="tpu_custom_call" | custom-call | flops 201326592 | bytes 1310720 | tf_op jit(solution)/shard_map/local_attn/pallas_call | solution.py:374
  42.3 0.7 %collective-permute-done.8.refs_1_ = f32[8,128]{1,0:T(8,128)S(1)} collective-permute-done((f32[8,128]{1,0:T(8,128)S(1)}, f32[8,128]{1,0:T(8,128)S(1)}, u32[]{:S(2)}, u32[]{:S(2)}) %collective-permute-start.8) | collective-permute-done | bytes 4128 | tf_op jit(solution)/shard_map/ppermute | solution.py:439
  43.0 0.4 spread.1
  43.5 1.6 %collective-permute-done.12.refs_1_.p_ref = f32[4,144,128]{2,1,0:T(8,128)S(1)} collective-permute-done((f32[4,144,128]{2,1,0:T(8,128)S(1)}, f32[4,144,128]{2,1,0:T(8,128)S(1)}, u32[]{:S(2)}, u32[]{:S(2)}) %collective-permute-start.12) | collective-permute-done | bytes 294944 | tf_op jit(solution)/shard_map/ppermute | solution.py:436
  45.0 0.7 %collective-permute-start.13 = (f32[2,16,128]{2,1,0:T(8,128)S(1)}, f32[2,16,128]{2,1,0:T(8,128)S(1)}, u32[]{:S(2)}, u32[]{:S(2)}) collective-permute-start(f32[2,16,128]{2,1,0:T(8,128)S(1)} %get-tuple-element.95), channel_id=1, source_target_pairs={{0,1},{1,0},{2,3},{3,2},{4,5},{5,4},{6,7},{7,6},{8,9},{9,8},{10,11... | collective-permute-start | bytes 49160 | tf_op jit(solution)/shard_map/ppermute | solution.py:439
  45.7 2.0 %last.2 = (bf16[1024,1024]{1,0:T(8,128)(2,1)}, f32[8,128]{1,0:T(8,128)S(1)}) custom-call(f32[1,1024]{1,0:T(1,128)S(1)} %bitcast.1, f32[4,128,128]{2,1,0:T(8,128)S(1)} %get-tuple-element.87.p_ref, f32[1024,128]{1,0:T(8,128)S(1)} %get-tuple-element.64.refs_4_.rest_0_, f32[1024,128]{1,0:T(8,128)S(1)} %get-tuple-element.65.refs_2_.rest_1_, ...), custom_call_target="tpu_custom_call" | custom-call | flops 402653184 | bytes 5242880 | tf_op jit(solution)/shard_map/last/pallas_call | solution.py:418
  47.7 1.1 %collective-permute-done.13.refs_0_ = f32[2,16,128]{2,1,0:T(8,128)S(1)} collective-permute-done((f32[2,16,128]{2,1,0:T(8,128)S(1)}, f32[2,16,128]{2,1,0:T(8,128)S(1)}, u32[]{:S(2)}, u32[]{:S(2)}) %collective-permute-start.13) | collective-permute-done | bytes 16416 | tf_op jit(solution)/shard_map/ppermute | solution.py:439
  48.8 3.0 %collective-permute-start.14 = (f32[16,128]{1,0:T(8,128)S(1)}, f32[16,128]{1,0:T(8,128)S(1)}, u32[]{:S(2)}, u32[]{:S(2)}) collective-permute-start(f32[16,128]{1,0:T(8,128)S(1)} %get-tuple-element.100), channel_id=1, source_target_pairs={{0,3},{1,2},{2,1},{3,0},{4,7},{5,6},{6,5},{7,4},{8,11},{9,10},{10,... | collective-permute-start | bytes 24584 | tf_op jit(solution)/shard_map/ppermute | solution.py:439
  51.8 2.0 %last.3 = (bf16[1024,1024]{1,0:T(8,128)(2,1)}, f32[8,128]{1,0:T(8,128)S(1)}) custom-call(f32[1,1024]{1,0:T(1,128)S(1)} %bitcast.2, f32[4,144,128]{2,1,0:T(8,128)S(1)} %collective-permute-done.12.refs_1_.p_ref, f32[1024,128]{1,0:T(8,128)S(1)} %get-tuple-element.70.refs_4_.rest_0_, ...), custom_call_target="tpu_custom_call", output_to_operand_aliasing={{0}: (10, {})} | custom-call | flops 402653184 | bytes 5242880 | tf_op jit(solution)/shard_map/last/pallas_call | solution.py:418
  53.8 0.6 %sum.1 = f32[16,128]{1,0:T(8,128)} custom-call(f32[16,128]{1,0:T(8,128)S(1)} %get-tuple-element.98.rest_9_.refs_0_, f32[16,128]{1,0:T(8,128)S(1)} %collective-permute-done.14.refs_1_, f32[8,128]{1,0:T(8,128)S(1)} %get-tuple-element.101.refs_2_), custom_call_target="tpu_custom_call" | custom-call | tf_op jit(solution)/shard_map/sum/pallas_call | solution.py:301
  (25 shorter events, 0.9 us)
Async XLA Ops:
  3.9 1.6 %collective-permute-start = (f32[4,136,128]{2,1,0:T(8,128)S(1)}, f32[4,136,128]{2,1,0:T(8,128)S(1)}, u32[]{:S(2)}, u32[]{:S(2)}) collective-permute-start(f32[4,136,128]{2,1,0:T(8,128)S(1)} %get-tuple-element.56), channel_id=1, source_target_pairs={{0,4},{4,0},{8,12},{12,8},{16,20},{20,16},{24,28},{28,24},{32,36},... | collective-permute-start | bytes 835592 | tf_op jit(solution)/shard_map/ppermute | solution.py:436
  4.0 1.0 %copy-start.1 = (f32[8,1024]{1,0:T(8,128)S(1)}, f32[8,1024]{1,0:T(8,128)}, u32[]{:S(2)}) copy-start(f32[8,1024]{1,0:T(8,128)} %refs_0_.6) | copy-start | bytes 98308
  4.0 5.8 %copy-start = (bf16[1024,1024]{1,0:T(8,128)(2,1)S(1)}, bf16[1024,1024]{1,0:T(8,128)(2,1)}, u32[]{:S(2)}) copy-start(bf16[1024,1024]{1,0:T(8,128)(2,1)} %refs_0_.11) | copy-start | bytes 6291460
  5.6 6.0 %collective-permute-start.2 = (f32[136,128]{1,0:T(8,128)S(1)}, f32[136,128]{1,0:T(8,128)S(1)}, u32[]{:S(2)}, u32[]{:S(2)}) collective-permute-start(f32[136,128]{1,0:T(8,128)S(1)} %get-tuple-element.60), channel_id=1, source_target_pairs={{0,16},{4,20},{8,24},{12,28},{16,0},{20,4},{24,8},{28,12},{32,48},... | collective-permute-start | bytes 208904 | tf_op jit(solution)/shard_map/ppermute | solution.py:436
  8.7 4.4 %collective-permute-start.3 = (f32[136,128]{1,0:T(8,128)S(1)}, f32[136,128]{1,0:T(8,128)S(1)}, u32[]{:S(2)}, u32[]{:S(2)}) collective-permute-start(f32[136,128]{1,0:T(8,128)S(1)} %get-tuple-element.61), channel_id=1, source_target_pairs={{0,8},{4,12},{8,0},{12,4},{16,24},{20,28},{24,16},{28,20},{32,40},... | collective-permute-start | bytes 208904 | tf_op jit(solution)/shard_map/ppermute | solution.py:436
  9.3 5.5 %collective-permute-start.4 = (f32[136,128]{1,0:T(8,128)S(1)}, f32[136,128]{1,0:T(8,128)S(1)}, u32[]{:S(2)}, u32[]{:S(2)}) collective-permute-start(f32[136,128]{1,0:T(8,128)S(1)} %get-tuple-element.62), channel_id=1, source_target_pairs={{0,24},{4,28},{8,16},{12,20},{16,8},{20,12},{24,0},{28,4},{32,56},... | collective-permute-start | bytes 208904 | tf_op jit(solution)/shard_map/ppermute | solution.py:436
  14.9 4.4 %collective-permute-start.5 = (f32[136,128]{1,0:T(8,128)S(1)}, f32[136,128]{1,0:T(8,128)S(1)}, u32[]{:S(2)}, u32[]{:S(2)}) collective-permute-start(f32[136,128]{1,0:T(8,128)S(1)} %slab.1.refs_5_.refs_0_), channel_id=1, source_target_pairs={{0,32},{4,36},{8,40},{12,44},{16,48},{20,52},{24,56},{28,60},{32,0... | collective-permute-start | bytes 208904 | tf_op jit(solution)/shard_map/ppermute | solution.py:436
  19.3 7.0 %collective-permute-start.6 = (f32[136,128]{1,0:T(8,128)S(1)}, f32[136,128]{1,0:T(8,128)S(1)}, u32[]{:S(2)}, u32[]{:S(2)}) collective-permute-start(f32[136,128]{1,0:T(8,128)S(1)} %get-tuple-element.67.refs_5_.refs_0_), channel_id=1, source_target_pairs={{0,64},{4,68},{8,72},{12,76},{16,80},{20,84},{24,88},{28,92},{32,9... | collective-permute-start | bytes 208904 | tf_op jit(solution)/shard_map/ppermute | solution.py:436
  22.6 3.7 %collective-permute-start.1 = (f32[8,128]{1,0:T(8,128)S(1)}, f32[8,128]{1,0:T(8,128)S(1)}, u32[]{:S(2)}, u32[]{:S(2)}) collective-permute-start(f32[8,128]{1,0:T(8,128)S(1)} %get-tuple-element.58.refs_0_), channel_id=1, source_target_pairs={{0,1},{1,0},{2,3},{3,2},{4,5},{5,4},{6,7},{7,6},{8,9},{9,8},{10,11... | collective-permute-start | bytes 12296 | tf_op jit(solution)/shard_map/ppermute | solution.py:439
  26.4 7.5 %collective-permute-start.7 = (f32[136,128]{1,0:T(8,128)S(1)}, f32[136,128]{1,0:T(8,128)S(1)}, u32[]{:S(2)}, u32[]{:S(2)}) collective-permute-start(f32[136,128]{1,0:T(8,128)S(1)} %get-tuple-element.71.refs_5_.refs_0_), channel_id=1, source_target_pairs={{0,192},{4,196},{8,200},{12,204},{16,208},{20,212},{24,216},{28,22... | collective-permute-start | bytes 208904 | tf_op jit(solution)/shard_map/ppermute | solution.py:436
  34.0 9.0 %collective-permute-start.9 = (f32[256,128]{1,0:T(8,128)S(1)}, f32[256,128]{1,0:T(8,128)S(1)}, u32[]{:S(2)}, u32[]{:S(2)}) collective-permute-start(f32[256,128]{1,0:T(8,128)S(1)} %get-tuple-element.78), channel_id=1, source_target_pairs={{0,16},{4,20},{8,24},{12,28},{16,0},{20,4},{24,8},{28,12},{32,48},... | collective-permute-start | bytes 393224 | tf_op jit(solution)/shard_map/ppermute | solution.py:436
  35.3 7.7 %collective-permute-start.10 = (f32[256,128]{1,0:T(8,128)S(1)}, f32[256,128]{1,0:T(8,128)S(1)}, u32[]{:S(2)}, u32[]{:S(2)}) collective-permute-start(f32[256,128]{1,0:T(8,128)S(1)} %get-tuple-element.79), channel_id=1, source_target_pairs={{0,8},{4,12},{8,0},{12,4},{16,24},{20,28},{24,16},{28,20},{32,40},... | collective-permute-start | bytes 393224 | tf_op jit(solution)/shard_map/ppermute | solution.py:436
  35.9 7.1 %collective-permute-start.11 = (f32[256,128]{1,0:T(8,128)S(1)}, f32[256,128]{1,0:T(8,128)S(1)}, u32[]{:S(2)}, u32[]{:S(2)}) collective-permute-start(f32[256,128]{1,0:T(8,128)S(1)} %get-tuple-element.80), channel_id=1, source_target_pairs={{0,24},{4,28},{8,16},{12,20},{16,8},{20,12},{24,0},{28,4},{32,56},... | collective-permute-start | bytes 393224 | tf_op jit(solution)/shard_map/ppermute | solution.py:436
  38.2 7.5 %copy-start.2 = (f32[1024]{0:T(1024)S(1)}, f32[1024]{0:T(1024)}, u32[]{:S(2)}) copy-start(f32[1024]{0:T(1024)} %param.10) | copy-start | bytes 12292
  38.2 4.8 %collective-permute-start.8 = (f32[8,128]{1,0:T(8,128)S(1)}, f32[8,128]{1,0:T(8,128)S(1)}, u32[]{:S(2)}, u32[]{:S(2)}) collective-permute-start(f32[8,128]{1,0:T(8,128)S(1)} %want.1.refs_0_), channel_id=1, source_target_pairs={{0,3},{1,2},{2,1},{3,0},{4,7},{5,6},{6,5},{7,4},{8,11},{9,10},{10,... | collective-permute-start | bytes 12296 | tf_op jit(solution)/shard_map/ppermute | solution.py:439
  43.4 1.7 %collective-permute-start.12 = (f32[4,144,128]{2,1,0:T(8,128)S(1)}, f32[4,144,128]{2,1,0:T(8,128)S(1)}, u32[]{:S(2)}, u32[]{:S(2)}) collective-permute-start(f32[4,144,128]{2,1,0:T(8,128)S(1)} %get-tuple-element.82), channel_id=1, source_target_pairs={{0,4},{4,0},{8,12},{12,8},{16,20},{20,16},{24,28},{28,24},{32,36},... | collective-permute-start | bytes 884744 | tf_op jit(solution)/shard_map/ppermute | solution.py:436
  45.0 3.7 %collective-permute-start.13 = (f32[2,16,128]{2,1,0:T(8,128)S(1)}, f32[2,16,128]{2,1,0:T(8,128)S(1)}, u32[]{:S(2)}, u32[]{:S(2)}) collective-permute-start(f32[2,16,128]{2,1,0:T(8,128)S(1)} %get-tuple-element.95), channel_id=1, source_target_pairs={{0,1},{1,0},{2,3},{3,2},{4,5},{5,4},{6,7},{7,6},{8,9},{9,8},{10,11... | collective-permute-start | bytes 49160 | tf_op jit(solution)/shard_map/ppermute | solution.py:439
  48.8 5.0 %collective-permute-start.14 = (f32[16,128]{1,0:T(8,128)S(1)}, f32[16,128]{1,0:T(8,128)S(1)}, u32[]{:S(2)}, u32[]{:S(2)}) collective-permute-start(f32[16,128]{1,0:T(8,128)S(1)} %get-tuple-element.100), channel_id=1, source_target_pairs={{0,3},{1,2},{2,1},{3,0},{4,7},{5,6},{6,5},{7,4},{8,11},{9,10},{10,... | collective-permute-start | bytes 24584 | tf_op jit(solution)/shard_map/ppermute | solution.py:439
